TPU v7x, 256 devices: a whole 4x4x8 slice. The times are simulated.
256 devices in a mesh: gx: 64 (over z, y, core), gy: 4 (over x).
Axes of the slice: x: 4, y: 4, z: 8, core: 2. Of those that a mesh axis runs over, the one named last changes fastest.
Arguments:
- body_load: float32 [64, 4, 6, 512], P('gx', 'gy'), may hold values from -54 to 54
- proximal: float32 [64, 4, 6, 512], P('gx', 'gy'), may hold values from 1 to 8
- contact_blocks: float32 [64, 4, 6, 12, 2048], P('gx', 'gy'), may hold values from -1.75 to 1.75
- slacks: float32 [64, 4, 6, 2048], P('gx', 'gy'), may hold values from 0.5 to 5
- dual_rows: float32 [64, 4, 6, 2048], P('gx', 'gy'), may hold values from 0.1 to 2
- first_body: int32 [64, 4, 2048], P('gx', 'gy'), may hold values from 0 to 511
- second_body: int32 [64, 4, 2048], P('gx', 'gy'), may hold values from 0 to 767
- border_bodies: int32 [64, 4, 8, 32], P('gx', 'gy'), may hold values from 0 to 511
Outputs:
- velocity_step: float32 [64, 4, 6, 512], P('gx', 'gy')
- residual: float32 [64, 4, 6, 512], P('gx', 'gy')
All inputs are finite; a program needn't handle non-finite values.
Results may differ from a plain program's by a relative error of at most 0.0003.
Values sent between devices are 32-bit elements; how exact they have to be, the bound alone decides.
A program may use at most 128 MiB of HBM per device.

v0:
```python
import jax
import jax.numpy as jnp
from jax import lax
from jax.sharding import PartitionSpec as P

ITERS = 4


HIGHEST = lax.Precision.HIGHEST


def with_halo(shard, sides, width):
    for axis, dim in sides:
        count, length = (lax.axis_size(axis), shard.shape[dim])
        up = [(i, (i + 1) % count) for i in range(count - 1)]
        down = [(j, i) for i, j in up]
        last = lax.slice_in_dim(shard, length - width, length, axis=dim)
        initial = lax.slice_in_dim(shard, 0, width, axis=dim)
        before = lax.ppermute(last, axis, up)
        after = lax.ppermute(initial, axis, down)
        shard = jnp.concatenate([before, shard, after], axis=dim)
    return shard


def deliver(buffers, block_pass):
    channels = buffers.shape[0]
    width_rows = buffers.shape[2]
    hollow = jnp.zeros((channels, 1, width_rows), buffers.dtype)
    tile_grid = jnp.concatenate([buffers[:, :4], hollow, buffers[:, 4:]], axis=1).reshape(
        channels, 3, 3, width_rows
    )
    if block_pass:
        padded = with_halo(tile_grid, (("gx", 1), ("gy", 2)), 1)
    else:
        padded = with_halo(tile_grid, (("gx", 1), ("gy", 2)), 1)
    arrived = padded[:, 0::2, 0::2]
    flattened = arrived.reshape(channels, 9, width_rows)
    return jnp.concatenate([flattened[:, :4], flattened[:, 5:]], axis=1)


def spread_ends(values, first_index, second_index, bodies, halo_slots):
    half_width = values.shape[0] // 2
    local_sums = (
        jnp.zeros((half_width, bodies), jnp.float32).at[:, first_index].add(values[:half_width])
    )
    extended = (
        jnp.zeros((half_width, bodies + halo_slots), jnp.float32)
        .at[:, second_index]
        .add(values[half_width:])
    )
    return (local_sums + extended[:, :bodies], extended[:, bodies:])


def cholesky_six(matrix):
    entries = {}
    for column in range(6):
        partial_sum = matrix[column, column]
        for inner_index in range(column):
            partial_sum = partial_sum - entries[column, inner_index] * entries[column, inner_index]
        pivot_value = jnp.sqrt(partial_sum)
        entries[column, column] = pivot_value
        for row_index in range(column + 1, 6):
            row_sum = matrix[row_index, column]
            for inner_index in range(column):
                row_sum = row_sum - entries[row_index, inner_index] * entries[column, inner_index]
            entries[row_index, column] = row_sum / pivot_value
    zero_row = jnp.zeros_like(matrix[0, 0])
    return jnp.stack(
        [
            jnp.stack([entries.get((row_index, column), zero_row) for column in range(6)])
            for row_index in range(6)
        ]
    )


def block_solve(factor, rows_in):
    forward = []
    for row_index in range(6):
        partial_sum = rows_in[row_index]
        for inner_index in range(row_index):
            partial_sum = partial_sum - factor[row_index, inner_index] * forward[inner_index]
        forward.append(partial_sum / factor[row_index, row_index])
    backward = [None] * 6
    for row_index in reversed(range(6)):
        partial_sum = forward[row_index]
        for inner_index in range(row_index + 1, 6):
            partial_sum = partial_sum - factor[inner_index, row_index] * backward[inner_index]
        backward[row_index] = partial_sum / factor[row_index, row_index]
    return jnp.stack(backward)


def weighted_norm(residual, preconditioned):
    return lax.psum(jnp.sum(residual * preconditioned), ("gx", "gy"))


def local(
    body_load, proximal, contact_blocks, slacks, dual_rows, first_body, second_body, border_bodies
):
    load_rows = body_load[0, 0]
    prox_rows = proximal[0, 0]
    blocks = contact_blocks[0, 0]
    scaling = dual_rows[0, 0] / slacks[0, 0]
    first_index = first_body[0, 0]
    second_index = second_body[0, 0]
    border = border_bodies[0, 0].reshape(-1)
    bodies = load_rows.shape[1]
    halo_slots = border.shape[0]
    stiffness = jnp.einsum("rac,rc,rbc->abc", blocks, scaling, blocks, precision=HIGHEST)
    upper_blocks = stiffness[:6, :6].reshape(36, -1)
    lower_blocks = stiffness[6:, 6:].reshape(36, -1)
    diag_local, diag_back = spread_ends(
        jnp.concatenate([upper_blocks, lower_blocks], axis=0),
        first_index,
        second_index,
        bodies,
        halo_slots,
    )
    returned = deliver(diag_back.reshape(36, 8, -1), True)
    diagonal = diag_local.at[:, border].add(returned.reshape(36, -1)).reshape(6, 6, bodies)
    diagonal = diagonal + prox_rows[:, None, :] * jnp.eye(6, dtype=jnp.float32)[:, :, None]
    factor = cholesky_six(diagonal)
    solution = jnp.zeros_like(load_rows)
    residual = load_rows
    preconditioned = block_solve(factor, residual)
    direction = preconditioned
    norm_now = weighted_norm(residual, preconditioned)
    for iteration in range(ITERS):
        sent_rows = jnp.take(direction, border, axis=1).reshape(6, 8, -1)
        halo_rows = deliver(sent_rows, False)
        extended = jnp.concatenate([direction, halo_rows.reshape(6, -1)], axis=1)
        stacked = jnp.concatenate(
            [jnp.take(direction, first_index, axis=1), jnp.take(extended, second_index, axis=1)],
            axis=0,
        )
        values = jnp.einsum("ijc,jc->ic", stiffness, stacked, precision=HIGHEST)
        image_local, image_back = spread_ends(values, first_index, second_index, bodies, halo_slots)
        back_rows = deliver(image_back.reshape(6, 8, -1), False)
        image_field = (
            image_local.at[:, border].add(back_rows.reshape(6, -1)) + prox_rows * direction
        )
        curvature = lax.psum(jnp.sum(direction * image_field), ("gx", "gy"))
        step_length = norm_now / curvature
        solution = solution + step_length * direction
        residual = residual - step_length * image_field
        preconditioned = block_solve(factor, residual)
        norm_next = weighted_norm(residual, preconditioned)
        direction = preconditioned + norm_next / norm_now * direction
        norm_now = norm_next
    return (solution[None, None], residual[None, None])


def solution(mesh):
    return jax.shard_map(
        local,
        mesh=mesh,
        in_specs=(
            P("gx", "gy", None, None),
            P("gx", "gy", None, None),
            P("gx", "gy", None, None, None),
            P("gx", "gy", None, None),
            P("gx", "gy", None, None),
            P("gx", "gy", None),
            P("gx", "gy", None),
            P("gx", "gy", None, None),
        ),
        out_specs=(P("gx", "gy", None, None), P("gx", "gy", None, None)),
        check_vma=False,
    )
```

profile of v0, /device:TPU:1, one launch (start us, length us, event | category | flops | bytes accessed | tf_op | source)
XLA Modules:
  0.0 1025.7 jit_solution(2449746619034689831)
XLA Ops:
  1.5 6.5 copy.767
  9.3 4.7 copy.623
  14.0 31.1 %convolution_bitcast_fusion = f32[12,12,2048]{0,1,2:T(8,128)} fusion(f32[6,12,2048]{1,0,2:T(8,128)} %copy.623, f32[1,1,6,12,2048]{3,2,4,0,1:T(8,128)} %copy.767), kind=kOutput, calls=%fused_computation.27 | convolution fusion | flops 21233664 | bytes 2359296 | tf_op jit(solution)/shard_map/rac,rc,rbc->abc/dot_general | solution.py:108
  45.1 15.8 %fusion.257 = (f32[6,6,2048]{0,1,2:T(8,128)}, f32[6,6,2048]{0,1,2:T(8,128)}) fusion(f32[12,12,2048]{0,1,2:T(8,128)} %convolution_bitcast_fusion), kind=kLoop, calls=%fused_computation.608 | loop fusion | bytes 1179648 | tf_op jit(solution)/shard_map/slice | solution.py:109
  60.8 5.3 copy.625
  66.6 11.7 %scatter_custom_fusion = f32[36,768]{0,1:T(8,128)S(1)} fusion(s32[2048]{0:T(1024)S(1)} %bitcast.1554, f32[2048,36]{1,0:T(8,128)S(1)} %copy.626, f32[]{:T(128)} %constant.28.clone.1), kind=kCustom, calls=%fused_computation.60 | custom fusion | flops 73728 | bytes 110596 | tf_op jit(solution)/shard_map/scatter-add | solution.py:49
  78.6 4.6 collective-permute-start
  85.4 3.2 collective-permute-done.1
  93.1 5.3 copy.627
  98.9 11.6 %scatter_fusion = f32[36,512]{0,1:T(8,128)S(1)} fusion(f32[36,512]{0,1:T(8,128)S(1)} %slice.846, s32[2048]{0:T(1024)S(1)} %bitcast.1531, f32[2048,36]{1,0:T(8,128)S(1)} %copy.628), kind=kCustom, calls=%fused_computation.13 | custom fusion | flops 73728 | bytes 892928 | tf_op jit(solution)/shard_map/scatter-add | solution.py:44
  119.2 5.5 gather_fusion
  124.7 4.0 collective-permute-start.6
  134.1 5.7 gather_fusion.2
  141.1 17.0 %fusion.285 = f32[2048,1,12]{2,1,0:T(1,128)S(1)} fusion(f32[12,2048,1]{0,2,1:T(1,128)S(1)} %copy.709, f32[12,12,2048]{0,1,2:T(8,128)} %convolution_bitcast_fusion), kind=kOutput, calls=%fused_computation.636 | convolution fusion | flops 3538944 | bytes 1376256 | tf_op jit(solution)/shard_map/ijc,jc->ic/dot_general | solution.py:135
  158.1 12.0 %scatter_custom_fusion.3 = f32[6,768]{0,1:T(8,128)S(1)} fusion(s32[2048]{0:T(1024)S(1)} %bitcast.1555, f32[12,2048]{0,1:T(8,128)S(1)} %bitcast.1427, f32[]{:T(128)} %constant.28.clone.1), kind=kCustom, calls=%fused_computation.44 | custom fusion | flops 12288 | bytes 1067012 | tf_op jit(solution)/shard_map/scatter-add | solution.py:49
  170.5 4.6 collective-permute-start.8
  185.4 11.6 %scatter_custom_fusion.4 = f32[6,512]{0,1:T(8,128)S(1)} fusion(f32[6,512]{0,1:T(8,128)S(1)} %copy.645, s32[2048]{0:T(1024)S(1)} %bitcast.1532, f32[12,2048]{0,1:T(8,128)S(1)} %bitcast.1428), kind=kCustom, calls=%fused_computation.42 | custom fusion | flops 12288 | bytes 1060864 | tf_op jit(solution)/shard_map/scatter-add | solution.py:44
  200.1 89.3 %all-reduce = (f32[]{:T(128)}, f32[]{:T(128)}) all-reduce(f32[]{:T(128)} %get-tuple-element.194, f32[]{:T(128)} %multiply_reduce_fusion), channel_id=1, replica_groups=mesh['gx'=64,'gy'=4] {'gx','gy'}, use_global_device_ids=true, to_apply=%region_4.0 | all-reduce | flops 2 | bytes 16 | tf_op jit(solution)/shard_map/psum | solution.py:93
  291.5 73.0 %psum.58 = f32[]{:T(128)} all-reduce(f32[]{:T(128)} %multiply_reduce_fusion.6), channel_id=1, replica_groups=mesh['gx'=64,'gy'=4] {'gx','gy'}, use_global_device_ids=true, to_apply=%region_11.15 | all-reduce | flops 1 | bytes 8 | tf_op jit(solution)/shard_map/psum | solution.py:93
  367.2 3.4 collective-permute-start.12
  372.5 5.5 gather_fusion.3
  385.2 5.5 gather_fusion.5
  392.0 17.0 %fusion.286 = f32[2048,1,12]{2,1,0:T(1,128)S(1)} fusion(f32[12,2048,1]{0,2,1:T(1,128)S(1)} %copy.711, f32[12,12,2048]{0,1,2:T(8,128)} %convolution_bitcast_fusion), kind=kOutput, calls=%fused_computation.637 | convolution fusion | flops 3538944 | bytes 1376256 | tf_op jit(solution)/shard_map/ijc,jc->ic/dot_general | solution.py:135
  409.0 12.0 %scatter_custom_fusion.6 = f32[6,768]{0,1:T(8,128)S(1)} fusion(s32[2048]{0:T(1024)S(1)} %bitcast.1556, f32[12,2048]{0,1:T(8,128)S(1)} %bitcast.1429, f32[]{:T(128)} %constant.28.clone.1), kind=kCustom, calls=%fused_computation.40 | custom fusion | flops 12288 | bytes 1067012 | tf_op jit(solution)/shard_map/scatter-add | solution.py:49
  421.4 4.2 collective-permute-start.16
  430.6 3.6 collective-permute-start.18
  435.7 11.6 %scatter_custom_fusion.7 = f32[6,512]{0,1:T(8,128)S(1)} fusion(f32[6,512]{0,1:T(8,128)S(1)} %copy.663, s32[2048]{0:T(1024)S(1)} %bitcast.1533, f32[12,2048]{0,1:T(8,128)S(1)} %bitcast.1430), kind=kCustom, calls=%fused_computation.38 | custom fusion | flops 12288 | bytes 1060864 | tf_op jit(solution)/shard_map/scatter-add | solution.py:44
  450.5 83.6 %psum.59 = f32[]{:T(128)} all-reduce(f32[]{:T(128)} %multiply_reduce_fusion.5), channel_id=1, replica_groups=mesh['gx'=64,'gy'=4] {'gx','gy'}, use_global_device_ids=true, to_apply=%region_16.20 | all-reduce | flops 1 | bytes 8 | tf_op jit(solution)/shard_map/psum | solution.py:141
  536.2 72.6 %psum.60 = f32[]{:T(128)} all-reduce(f32[]{:T(128)} %multiply_reduce_fusion.4), channel_id=1, replica_groups=mesh['gx'=64,'gy'=4] {'gx','gy'}, use_global_device_ids=true, to_apply=%region_18.22 | all-reduce | flops 1 | bytes 8 | tf_op jit(solution)/shard_map/psum | solution.py:93
  611.4 3.4 collective-permute-start.20
  616.8 5.5 gather_fusion.6
  629.5 5.5 gather_fusion.8
  636.3 17.0 %fusion.287 = f32[2048,1,12]{2,1,0:T(1,128)S(1)} fusion(f32[12,2048,1]{0,2,1:T(1,128)S(1)} %copy.713, f32[12,12,2048]{0,1,2:T(8,128)} %convolution_bitcast_fusion), kind=kOutput, calls=%fused_computation.638 | convolution fusion | flops 3538944 | bytes 1376256 | tf_op jit(solution)/shard_map/ijc,jc->ic/dot_general | solution.py:135
  653.4 12.0 %scatter_custom_fusion.9 = f32[6,768]{0,1:T(8,128)S(1)} fusion(s32[2048]{0:T(1024)S(1)} %bitcast.1557, f32[12,2048]{0,1:T(8,128)S(1)} %bitcast.1431, f32[]{:T(128)} %constant.28.clone.1), kind=kCustom, calls=%fused_computation.36 | custom fusion | flops 12288 | bytes 1067012 | tf_op jit(solution)/shard_map/scatter-add | solution.py:49
  665.7 4.2 collective-permute-start.24
  675.0 3.6 collective-permute-start.26
  680.0 11.8 %scatter_custom_fusion.10 = f32[6,512]{0,1:T(8,128)S(1)} fusion(f32[6,512]{0,1:T(8,128)S(1)} %copy.681, s32[2048]{0:T(1024)S(1)} %bitcast.1534, f32[12,2048]{0,1:T(8,128)S(1)} %bitcast.1432), kind=kCustom, calls=%fused_computation.34 | custom fusion | flops 12288 | bytes 1060864 | tf_op jit(solution)/shard_map/scatter-add | solution.py:44
  694.9 83.6 %psum.61 = f32[]{:T(128)} all-reduce(f32[]{:T(128)} %multiply_reduce_fusion.3), channel_id=1, replica_groups=mesh['gx'=64,'gy'=4] {'gx','gy'}, use_global_device_ids=true, to_apply=%region_23.27 | all-reduce | flops 1 | bytes 8 | tf_op jit(solution)/shard_map/psum | solution.py:141
  780.6 72.6 %psum.62 = f32[]{:T(128)} all-reduce(f32[]{:T(128)} %multiply_reduce_fusion.2), channel_id=1, replica_groups=mesh['gx'=64,'gy'=4] {'gx','gy'}, use_global_device_ids=true, to_apply=%region_25.29 | all-reduce | flops 1 | bytes 8 | tf_op jit(solution)/shard_map/psum | solution.py:93
  855.8 3.4 collective-permute-start.28
  861.2 5.5 gather_fusion.9
  873.9 5.5 gather_fusion.11
  880.7 17.0 %fusion.288 = f32[2048,1,12]{2,1,0:T(1,128)S(1)} fusion(f32[12,2048,1]{0,2,1:T(1,128)S(1)} %copy.715, f32[12,12,2048]{0,1,2:T(8,128)} %convolution_bitcast_fusion), kind=kOutput, calls=%fused_computation.639 | convolution fusion | flops 3538944 | bytes 1376256 | tf_op jit(solution)/shard_map/ijc,jc->ic/dot_general | solution.py:135
  897.8 12.0 %scatter_custom_fusion.12 = f32[6,768]{0,1:T(8,128)S(1)} fusion(s32[2048]{0:T(1024)S(1)} %bitcast.1558, f32[12,2048]{0,1:T(8,128)S(1)} %bitcast.1425, f32[]{:T(128)} %constant.28.clone.1), kind=kCustom, calls=%fused_computation.32 | custom fusion | flops 12288 | bytes 1067012 | tf_op jit(solution)/shard_map/scatter-add | solution.py:49
  910.1 4.2 collective-permute-start.32
  919.4 3.6 collective-permute-start.34
  924.4 11.6 %scatter_custom_fusion.13 = f32[6,512]{0,1:T(8,128)S(1)} fusion(f32[6,512]{0,1:T(8,128)S(1)} %copy.699, s32[2048]{0:T(1024)S(1)} %bitcast.1535, f32[12,2048]{0,1:T(8,128)S(1)} %bitcast.1426), kind=kCustom, calls=%fused_computation.30 | custom fusion | flops 12288 | bytes 1060864 | tf_op jit(solution)/shard_map/scatter-add | solution.py:44
  939.1 83.6 %psum.63 = f32[]{:T(128)} all-reduce(f32[]{:T(128)} %multiply_reduce_fusion.1), channel_id=1, replica_groups=mesh['gx'=64,'gy'=4] {'gx','gy'}, use_global_device_ids=true, to_apply=%region_30.34 | all-reduce | flops 1 | bytes 8 | tf_op jit(solution)/shard_map/psum | solution.py:141
  (331 shorter events, 106.0 us)
Async XLA Ops:
  45.1 21.5 %copy-start.2 = (s32[1,1,2048]{2,1,0:T(1,128)S(1)}, s32[1,1,2048]{2,1,0:T(1,128)}, u32[]{:S(2)}) copy-start(s32[1,1,2048]{2,1,0:T(1,128)} %param.20) | copy-start | bytes 24580
  45.1 40.0 %copy-start.4 = (s32[1,1,8,32]{3,2,1,0:T(8,128)S(1)}, s32[1,1,8,32]{3,2,1,0:T(8,128)}, u32[]{:S(2)}) copy-start(s32[1,1,8,32]{3,2,1,0:T(8,128)} %param.21) | copy-start | bytes 3076
  45.1 40.2 %copy-start.3 = (s32[1,1,2048]{2,1,0:T(1,128)S(1)}, s32[1,1,2048]{2,1,0:T(1,128)}, u32[]{:S(2)}) copy-start(s32[1,1,2048]{2,1,0:T(1,128)} %param.19) | copy-start | bytes 24580
  60.8 38.0 %copy-start = (f32[1,1,6,512]{3,1,2,0:T(1,128)S(1)}, f32[1,1,6,512]{3,1,2,0:T(1,128)}, u32[]{:S(2)}) copy-start(f32[1,1,6,512]{3,1,2,0:T(1,128)} %param.15) | copy-start | bytes 36868
  60.8 52.6 %copy-start.1 = (f32[1,1,6,512]{3,1,2,0:T(1,128)S(1)}, f32[1,1,6,512]{3,1,2,0:T(1,128)}, u32[]{:S(2)}) copy-start(f32[1,1,6,512]{3,1,2,0:T(1,128)} %param.14) | copy-start | bytes 36868
  78.6 6.8 collective-permute-start
  83.2 5.4 collective-permute-start.1
  88.6 21.9 %collective-permute-start.2 = (f32[36,5,1,32]{0,3,2,1:T(8,128)S(1)}, f32[36,5,1,32]{0,3,2,1:T(8,128)S(1)}, u32[]{:S(2)}, u32[]{:S(2)}) collective-permute-start(f32[36,5,1,32]{0,3,2,1:T(8,128)S(1)} %get-tuple-element.104), channel_id=1, source_target_pairs={{0,1},{1,2},{2,3},{4,5},{5,6},{6,7},{8,9},{9,10},{10,11},{12,13},{... | collective-permute-start | bytes 69128 | tf_op jit(solution)/shard_map/ppermute | solution.py:19
  91.7 18.8 %collective-permute-start.3 = (f32[36,5,1,32]{0,3,2,1:T(8,128)S(1)}, f32[36,5,1,32]{0,3,2,1:T(8,128)S(1)}, u32[]{:S(2)}, u32[]{:S(2)}) collective-permute-start(f32[36,5,1,32]{0,3,2,1:T(8,128)S(1)} %get-tuple-element.105), channel_id=1, source_target_pairs={{1,0},{2,1},{3,2},{5,4},{6,5},{7,6},{9,8},{10,9},{11,10},{13,12},{... | collective-permute-start | bytes 69128 | tf_op jit(solution)/shard_map/ppermute | solution.py:20
  114.8 9.8 collective-permute-start.4
  117.0 7.7 collective-permute-start.5
  124.7 6.0 collective-permute-start.6
  128.7 5.0 collective-permute-start.7
  170.5 6.7 collective-permute-start.8
  175.2 5.0 collective-permute-start.9
  180.2 16.8 %collective-permute-start.10 = (f32[6,5,1,32]{3,0,2,1:T(8,128)S(1)}, f32[6,5,1,32]{3,0,2,1:T(8,128)S(1)}, u32[]{:S(2)}, u32[]{:S(2)}) collective-permute-start(f32[6,5,1,32]{3,0,2,1:T(8,128)S(1)} %get-tuple-element.158), channel_id=1, source_target_pairs={{0,1},{1,2},{2,3},{4,5},{5,6},{6,7},{8,9},{9,10},{10,11},{12,13},{... | collective-permute-start | bytes 11528 | tf_op jit(solution)/shard_map/ppermute | solution.py:19
  183.3 13.7 %collective-permute-start.11 = (f32[6,5,1,32]{3,0,2,1:T(8,128)S(1)}, f32[6,5,1,32]{3,0,2,1:T(8,128)S(1)}, u32[]{:S(2)}, u32[]{:S(2)}) collective-permute-start(f32[6,5,1,32]{3,0,2,1:T(8,128)S(1)} %get-tuple-element.159), channel_id=1, source_target_pairs={{1,0},{2,1},{3,2},{5,4},{6,5},{7,6},{9,8},{10,9},{11,10},{13,12},{... | collective-permute-start | bytes 11528 | tf_op jit(solution)/shard_map/ppermute | solution.py:20
  367.2 10.8 %collective-permute-start.12 = (f32[6,1,3,32]{3,0,2,1:T(8,128)S(1)}, f32[6,1,3,32]{3,0,2,1:T(8,128)S(1)}, u32[]{:S(2)}, u32[]{:S(2)}) collective-permute-start(f32[6,1,3,32]{3,0,2,1:T(8,128)S(1)} %get-tuple-element.184), channel_id=1, source_target_pairs={{0,4},{4,8},{8,12},{12,16},{16,20},{20,24},{24,28},{28,32},{32,36}... | collective-permute-start | bytes 6920 | tf_op jit(solution)/shard_map/ppermute | solution.py:19
  370.6 7.4 collective-permute-start.13
  378.0 3.8 collective-permute-start.14
  379.9 4.9 collective-permute-start.15
  421.4 6.3 collective-permute-start.16
  425.6 5.0 collective-permute-start.17
  430.6 16.7 %collective-permute-start.18 = (f32[6,5,1,32]{3,0,2,1:T(8,128)S(1)}, f32[6,5,1,32]{3,0,2,1:T(8,128)S(1)}, u32[]{:S(2)}, u32[]{:S(2)}) collective-permute-start(f32[6,5,1,32]{3,0,2,1:T(8,128)S(1)} %get-tuple-element.154), channel_id=1, source_target_pairs={{0,1},{1,2},{2,3},{4,5},{5,6},{6,7},{8,9},{9,10},{10,11},{12,13},{... | collective-permute-start | bytes 11528 | tf_op jit(solution)/shard_map/ppermute | solution.py:19
  434.2 13.1 %collective-permute-start.19 = (f32[6,5,1,32]{3,0,2,1:T(8,128)S(1)}, f32[6,5,1,32]{3,0,2,1:T(8,128)S(1)}, u32[]{:S(2)}, u32[]{:S(2)}) collective-permute-start(f32[6,5,1,32]{3,0,2,1:T(8,128)S(1)} %get-tuple-element.155), channel_id=1, source_target_pairs={{1,0},{2,1},{3,2},{5,4},{6,5},{7,6},{9,8},{10,9},{11,10},{13,12},{... | collective-permute-start | bytes 11528 | tf_op jit(solution)/shard_map/ppermute | solution.py:20
  611.4 10.9 %collective-permute-start.20 = (f32[6,1,3,32]{3,0,2,1:T(8,128)S(1)}, f32[6,1,3,32]{3,0,2,1:T(8,128)S(1)}, u32[]{:S(2)}, u32[]{:S(2)}) collective-permute-start(f32[6,1,3,32]{3,0,2,1:T(8,128)S(1)} %get-tuple-element.176), channel_id=1, source_target_pairs={{0,4},{4,8},{8,12},{12,16},{16,20},{20,24},{24,28},{28,32},{32,36}... | collective-permute-start | bytes 6920 | tf_op jit(solution)/shard_map/ppermute | solution.py:19
  614.9 7.4 collective-permute-start.21
  622.3 3.9 collective-permute-start.22
  624.2 4.9 collective-permute-start.23
  665.7 6.3 collective-permute-start.24
  669.9 5.0 collective-permute-start.25
  675.0 16.9 %collective-permute-start.26 = (f32[6,5,1,32]{3,0,2,1:T(8,128)S(1)}, f32[6,5,1,32]{3,0,2,1:T(8,128)S(1)}, u32[]{:S(2)}, u32[]{:S(2)}) collective-permute-start(f32[6,5,1,32]{3,0,2,1:T(8,128)S(1)} %get-tuple-element.150), channel_id=1, source_target_pairs={{0,1},{1,2},{2,3},{4,5},{5,6},{6,7},{8,9},{9,10},{10,11},{12,13},{... | collective-permute-start | bytes 11528 | tf_op jit(solution)/shard_map/ppermute | solution.py:19
  678.6 13.3 %collective-permute-start.27 = (f32[6,5,1,32]{3,0,2,1:T(8,128)S(1)}, f32[6,5,1,32]{3,0,2,1:T(8,128)S(1)}, u32[]{:S(2)}, u32[]{:S(2)}) collective-permute-start(f32[6,5,1,32]{3,0,2,1:T(8,128)S(1)} %get-tuple-element.151), channel_id=1, source_target_pairs={{1,0},{2,1},{3,2},{5,4},{6,5},{7,6},{9,8},{10,9},{11,10},{13,12},{... | collective-permute-start | bytes 11528 | tf_op jit(solution)/shard_map/ppermute | solution.py:20
  855.8 10.9 %collective-permute-start.28 = (f32[6,1,3,32]{3,0,2,1:T(8,128)S(1)}, f32[6,1,3,32]{3,0,2,1:T(8,128)S(1)}, u32[]{:S(2)}, u32[]{:S(2)}) collective-permute-start(f32[6,1,3,32]{3,0,2,1:T(8,128)S(1)} %get-tuple-element.168), channel_id=1, source_target_pairs={{0,4},{4,8},{8,12},{12,16},{16,20},{20,24},{24,28},{28,32},{32,36}... | collective-permute-start | bytes 6920 | tf_op jit(solution)/shard_map/ppermute | solution.py:19
  859.3 7.5 collective-permute-start.29
  866.8 3.9 collective-permute-start.30
  868.6 4.9 collective-permute-start.31
  910.1 6.4 collective-permute-start.32
  914.4 5.0 collective-permute-start.33
  919.4 16.7 %collective-permute-start.34 = (f32[6,5,1,32]{3,0,2,1:T(8,128)S(1)}, f32[6,5,1,32]{3,0,2,1:T(8,128)S(1)}, u32[]{:S(2)}, u32[]{:S(2)}) collective-permute-start(f32[6,5,1,32]{3,0,2,1:T(8,128)S(1)} %get-tuple-element.146), channel_id=1, source_target_pairs={{0,1},{1,2},{2,3},{4,5},{5,6},{6,7},{8,9},{9,10},{10,11},{12,13},{... | collective-permute-start | bytes 11528 | tf_op jit(solution)/shard_map/ppermute | solution.py:19
  923.0 13.1 %collective-permute-start.35 = (f32[6,5,1,32]{3,0,2,1:T(8,128)S(1)}, f32[6,5,1,32]{3,0,2,1:T(8,128)S(1)}, u32[]{:S(2)}, u32[]{:S(2)}) collective-permute-start(f32[6,5,1,32]{3,0,2,1:T(8,128)S(1)} %get-tuple-element.147), channel_id=1, source_target_pairs={{1,0},{2,1},{3,2},{5,4},{6,5},{7,6},{9,8},{10,9},{11,10},{13,12},{... | collective-permute-start | bytes 11528 | tf_op jit(solution)/shard_map/ppermute | solution.py:20
where the time goes:
time: 1040 us; the launch traced here: 1030 us
  blocking collectives  558 us (54%)
  other arithmetic  141 us (14%)
  matrix products  99.3 us (10%)
  local copies, waits for them, and re-layouts  98 us (9%)
  starting transfers between devices  90.1 us (9%)
  waiting for transfers between devices  26.7 us (3%)
  between operations  12.4 us (1%)
    psum x4, blocking collectives, weighted_norm(): return lax.psum(jnp.sum(residual * preconditioned), ('gx', 'gy'))  307 us
    psum x3, blocking collectives, local(): curvature = lax.psum(jnp.sum(direction * image_field), ('gx', 'gy'))  251 us
    dot_general x4, matrix products, local(): values = jnp.einsum('ijc,jc->ic', stiffness, stacked, precision=HIGHEST)  68.2 us
    ppermute x18, starting transfers between devices, with_halo(): before = lax.ppermute(last, axis, up)  61 us
    scatter-add x5, other arithmetic, spread_ends(): extended = jnp.zeros((half_width, bodies + halo_slots), jnp.float32).at[:...  59.9 us
    scatter-add x5, other arithmetic, spread_ends(): jnp.zeros((half_width, bodies), jnp.float32).at[:, first_index]  58.3 us
    dot_general x1, matrix products, local(): jnp.einsum('rac,rc,rbc->abc', blocks, scaling, blocks, precision=HIGHEST)  31.1 us
    ppermute x18, starting transfers between devices, with_halo(): after = lax.ppermute(initial, axis, down)  29.1 us
  transfers between devices with their start and end apart: 36, of which 9 were waited for; matrix products, arithmetic and copies ran while one was open for 9% of the time, Pallas kernels for 0%

commit v1 on v0

v1 whole, which is shorter than its diff:
```python
import functools

import jax
import jax.numpy as jnp
from jax import lax
from jax.experimental import pallas as pl
from jax.experimental.pallas import tpu as pltpu
from jax.sharding import PartitionSpec as P

ITERS = 4
LANES = 128
ROWS = 8
SPAN = 256
GROUP = 512
SPLITS = 3
MESH = pl.DeviceIdType.MESH
OFFSETS = ((-1, -1), (-1, 0), (-1, 1), (0, -1), (0, 1), (1, -1), (1, 0), (1, 1))


def gather_columns(chunks, lane, chunk_of):
    picked = jnp.take_along_axis(chunks[0], lane, axis=1, mode="promise_in_bounds")
    for number in range(1, len(chunks)):
        other = jnp.take_along_axis(chunks[number], lane, axis=1, mode="promise_in_bounds")
        picked = jnp.where(chunk_of == number, other, picked)
    return picked


def split_terms(values):
    terms = []
    for number in range(SPLITS):
        term = values.astype(jnp.bfloat16).astype(jnp.float32)
        terms.append(term)
        if number + 1 < SPLITS:
            values = values - term
    return terms


def one_hot_dot(left, hot):
    return lax.dot_general(
        left, hot, (((1,), (1,)), ((), ())), preferred_element_type=jnp.float32
    )


def sum_rows(values):
    for shift in (4, 2, 1):
        values = values + pltpu.roll(values, shift, 0)
    return values


def wide(ref_value, lanes):
    return jnp.broadcast_to(ref_value, (ROWS, lanes))


def inverse_six(entry, width):
    lower, pivots = {}, []
    for column in range(6):
        scaled = [lower[column, inner] * pivots[inner][0] for inner in range(column)]
        value = entry(column, column)
        for inner in range(column):
            value = value - scaled[inner] * lower[column, inner]
        flipped = 1.0 / value
        pivots.append((value, flipped))
        for row in range(column + 1, 6):
            value = entry(row, column)
            for inner in range(column):
                value = value - lower[row, inner] * scaled[inner]
            lower[row, column] = value * flipped
    unit = {}
    for column in range(6):
        for row in range(column + 1, 6):
            value = -lower[row, column]
            for inner in range(column + 1, row):
                value = value - lower[row, inner] * unit[inner, column]
            unit[row, column] = value
    result = {}
    for row in range(6):
        for column in range(row + 1):
            value = None
            for inner in range(row, 6):
                left = pivots[inner][1]
                if inner > row:
                    left = left * unit[inner, row]
                if inner > column:
                    left = left * unit[inner, column]
                value = left if value is None else value + left
            result[row, column] = result[column, row] = value
    return result


def coefficients(moments):
    def inner(left, right):
        total = None
        for i, a in enumerate(left):
            for j, b in enumerate(right):
                term = a * b * moments[i + j]
                total = term if total is None else total + term
        return total

    one = jnp.ones_like(moments[0])
    step = [None] * ITERS
    residual, direction = [one], [one]
    norm_now = moments[0]
    for iteration in range(ITERS):
        image = []
        for j in range(len(direction) + 1):
            parts = [direction[i] for i in (j - 1, j) if 0 <= i < len(direction)]
            image.append(sum(parts[1:], parts[0]))
        length = norm_now / inner(direction, image)
        for j, value in enumerate(direction):
            step[j] = length * value if step[j] is None else step[j] + length * value
        residual = [
            (residual[j] - length * image[j]) if j < len(residual) else -length * image[j]
            for j in range(len(image))
        ]
        if iteration + 1 < ITERS:
            norm_next = inner(residual, residual)
            ratio = norm_next / norm_now
            direction = [
                (residual[j] + ratio * direction[j]) if j < len(direction) else residual[j]
                for j in range(len(residual))
            ]
            norm_now = norm_next
    return step, residual


def kernel(
    sizes,
    load_ref, prox_ref, block_ref, slack_ref, dual_ref, first_ref, second_ref, border_ref,
    step_ref, residual_ref,
    g1, g2, hot1, hot2, hotb, lane1, lane2, chunk1, chunk2, laneb, chunkb,
    left1, left2, leftb, basis_v, basis_q, prox8, inverse, diag, border_pad,
    diag_send, diag_recv, fore_send, fore_recv, back_send, back_recv,
    moment, part_recv, whole_send, whole_recv,
    diag_ssem, diag_rsem, fore_ssem, fore_rsem, back_ssem, back_rsem,
    part_ssem, part_rsem, whole_ssem, whole_rsem,
):
    nx, ny, ys, zs = sizes
    bodies, contacts = load_ref.shape[1], block_ref.shape[2]
    spans = bodies // SPAN
    chunks = bodies // LANES
    gx, gy = lax.axis_index("gx"), lax.axis_index("gy")
    z_at, y_at, core = gx // (2 * ys), (gx // 2) % ys, gx % 2

    near = [((gx + dx + nx) % nx, (gy + dy + ny) % ny) for dx, dy in OFFSETS]
    real = []
    for dx, dy in OFFSETS:
        to_x, to_y = gx + dx, gy + dy
        real.append((to_x >= 0) & (to_x < nx) & (to_y >= 0) & (to_y < ny))
    part_count, whole_count = ny * ys, zs * 2
    part_near, whole_near = [], []
    for offset in range(1, part_count):
        other = (gy * ys + y_at + offset) % part_count
        part_near.append((z_at * 2 * ys + (other % ys) * 2 + core, other // ys))
    for offset in range(1, whole_count):
        other = (z_at * 2 + core + offset) % whole_count
        whole_near.append(((other // 2) * 2 * ys + y_at * 2 + other % 2, gy))

    barrier = pltpu.get_barrier_semaphore()
    everyone = near + part_near + whole_near
    for device in everyone:
        pl.semaphore_signal(barrier, inc=1, device_id=device, device_id_type=MESH)

    first = wide(first_ref[...], contacts)
    second = wide(second_ref[...], contacts)
    lane1[...] = first % LANES
    chunk1[...] = first // LANES
    lane2[...] = second % LANES
    chunk2[...] = second // LANES
    border_pad[...] = jnp.zeros_like(border_pad)
    border_pad[:, : border_ref.shape[1]] = border_ref[...]
    lane_group = lax.broadcasted_iota(jnp.int32, (1, LANES), 1) // 32
    row_at = [border_pad[7 - place : 8 - place, :] for place in range(8)]
    border_rows = []
    for half in range(2):
        row = row_at[4 * half]
        for quarter in range(1, 4):
            row = jnp.where(
                lane_group == quarter,
                pltpu.roll(row_at[4 * half + quarter], 32 * quarter, 1),
                row,
            )
        border_rows.append(row)
    border = wide(jnp.concatenate(border_rows, axis=1), 2 * LANES)
    laneb[...] = border % LANES
    chunkb[...] = border // LANES

    for hot, index, count in ((hot1, first_ref[...], contacts), (hot2, second_ref[...], contacts)):
        for at in range(0, count, GROUP):
            spot = index[:, at : at + GROUP] % SPAN
            rows = lax.broadcasted_iota(jnp.int32, (SPAN, GROUP), 0)
            hot[:, at : at + GROUP] = jnp.where(rows == spot, 1.0, 0.0).astype(jnp.bfloat16)
    rows = lax.broadcasted_iota(jnp.int32, (SPAN, 2 * LANES), 0)
    hotb[...] = jnp.where(rows == border[0:1] % SPAN, 1.0, 0.0).astype(jnp.bfloat16)

    root = jnp.sqrt(dual_ref[...] / slack_ref[...])
    for r in range(6):
        head = block_ref[r, 0:8, :] * root[r : r + 1]
        tail = block_ref[r, 8:12, :] * root[r : r + 1]
        g1[r] = jnp.concatenate([head[0:6], head[0:2]], axis=0)
        g2[r] = jnp.concatenate([head[6:8], tail, head[6:8]], axis=0)
    zero_rows = jnp.zeros((2, bodies), jnp.float32)
    prox8[...] = jnp.concatenate([prox_ref[...], zero_rows], axis=0)
    basis_q[0] = jnp.concatenate([load_ref[...], zero_rows], axis=0)

    def put_first(target, at, base, values, span_of, width):
        for term in split_terms(values):
            masked = [jnp.where(span_of == s, term, 0.0) for s in range(spans)]
            target[base : base + ROWS * spans, at : at + width] = jnp.concatenate(
                masked, axis=0
            ).astype(jnp.bfloat16)
            base += ROWS * spans
        return base

    def put_second(target, at, base, values, span_of, width):
        base = put_first(target, at, base, values, span_of, width)
        terms = [jnp.where(span_of == spans, t, 0.0) for t in split_terms(values)]
        if len(terms) % 2:
            terms.append(jnp.zeros_like(terms[0]))
        target[base : base + ROWS * len(terms), at : at + width] = jnp.concatenate(
            terms, axis=0
        ).astype(jnp.bfloat16)
        return base + ROWS * len(terms)

    local_rows = ROWS * spans * SPLITS

    def local_sum(product, base):
        columns = []
        for s in range(spans):
            total = product[base + ROWS * s : base + ROWS * (s + 1)]
            for number in range(1, SPLITS):
                start = base + ROWS * (number * spans + s)
                total = total + product[start : start + ROWS]
            columns.append(total)
        return jnp.concatenate(columns, axis=1)

    def halo_sum(product, base):
        total = product[base : base + ROWS]
        for number in range(1, SPLITS):
            total = total + product[base + ROWS * number : base + ROWS * (number + 1)]
        return total

    def arrange(slots, place_of):
        halves = [None, None]
        for k in range(8):
            place = place_of(k)
            code = jnp.where(real[k], place % 4, -1)
            piece = jnp.where(lane_group == code, slots(k), 0.0)
            half = place // 4
            halves[half] = piece if halves[half] is None else halves[half] + piece
        return jnp.concatenate(halves, axis=1)

    def exchange(send, recv, ssem, rsem, place_of):
        copies = []
        for k, device in enumerate(near):
            copies.append(
                pltpu.make_async_remote_copy(
                    src_ref=send.at[place_of(k) // 4],
                    dst_ref=recv.at[7 - k],
                    send_sem=ssem.at[k],
                    recv_sem=rsem.at[7 - k],
                    device_id=device,
                    device_id_type=MESH,
                )
            )
            copies[-1].start()
        return copies

    def settle(copies):
        for copy in copies:
            copy.wait_send()
        for copy in copies:
            copy.wait_recv()

    reverse = lambda k: 7 - k
    forward = lambda k: k

    sub = lax.broadcasted_iota(jnp.int32, (ROWS, GROUP), 0)
    per_first, per_second = local_rows, left2.shape[0] // 3
    for at in range(0, contacts, GROUP):
        cols = slice(at, at + GROUP)
        for source, target, chunk_ref, put, per in (
            (g1, left1, chunk1, put_first, per_first),
            (g2, left2, chunk2, put_second, per_second),
        ):
            sums = [None] * 4
            for r in range(6):
                value = source[r, :, cols]
                for d in range(4):
                    term = value * (pltpu.roll(value, ROWS - d, 0) if d else value)
                    sums[d] = term if sums[d] is None else sums[d] + term
            span_of = chunk_ref[:, cols] // 2
            for d in range(3):
                packed = jnp.where(sub == 6, pltpu.roll(sums[3], 6 - d, 0), sums[d])
                put(target, at, d * per, packed, span_of, GROUP)
    product2 = one_hot_dot(left2[...], hot2[...])
    for d in range(3):
        halo = halo_sum(product2, d * per_second + local_rows)
        diag_send[0, d * ROWS : (d + 1) * ROWS, :] = halo[:, :LANES]
        diag_send[1, d * ROWS : (d + 1) * ROWS, :] = halo[:, LANES:]
    pl.semaphore_wait(barrier, len(everyone))
    copies = exchange(diag_send, diag_recv, diag_ssem, diag_rsem, forward)
    product1 = one_hot_dot(left1[...], hot1[...])
    for d in range(3):
        diag[d * ROWS : (d + 1) * ROWS, :] = local_sum(product1, d * per_first) + local_sum(
            product2, d * per_second
        )
    settle(copies)
    span_b = chunkb[...] // 2
    for d in range(3):
        returned = arrange(lambda k: diag_recv[k, d * ROWS : (d + 1) * ROWS, :], reverse)
        put_first(leftb, 0, d * per_first, returned, span_b, 2 * LANES)
    product = one_hot_dot(leftb[...], hotb[...])
    for d in range(3):
        rows = slice(d * ROWS, (d + 1) * ROWS)
        total = diag[rows, :] + local_sum(product, d * per_first)
        diag[rows, :] = total + prox8[...] if d == 0 else total

    def entry(row, column):
        d = (column - row) % 6
        if d == 3:
            at = min(row, column) * ROWS + 6
        elif d < 3:
            at = d * ROWS + row
        else:
            at = (6 - d) * ROWS + column
        return diag[at : at + 1, :]

    inverse[...] = jnp.zeros_like(inverse)
    for (row, column), value in inverse_six(entry, bodies).items():
        inverse[column, row : row + 1, :] = value

    def precondition(field):
        total = None
        for b in range(6):
            term = inverse[b] * wide(field[b : b + 1, :], bodies)
            total = term if total is None else total + term
        return total

    def dot_rows(left, right):
        product = left * right
        total = product[:, 0:LANES]
        for at in range(LANES, bodies, LANES):
            total = total + product[:, at : at + LANES]
        return total

    def cut(field, count):
        return [field[:, i * LANES : (i + 1) * LANES] for i in range(count)]

    basis_v[0] = precondition(basis_q[0])
    pending = []
    for k in range(ITERS):
        v_now, q_now = basis_v[k], basis_q[k]
        parts = cut(v_now, chunks)
        for half in range(2):
            cols = slice(half * LANES, (half + 1) * LANES)
            fore_send[k, half] = gather_columns(parts, laneb[:, cols], chunkb[:, cols])
        copies = exchange(fore_send.at[k], fore_recv.at[k], fore_ssem.at[k], fore_rsem.at[k], reverse)
        moment[2 * k : 2 * k + 1, :] = sum_rows(dot_rows(v_now, q_now))[0:1]
        settle(copies)
        extended = parts + cut(arrange(lambda s: fore_recv[k, s], forward), 2)
        energy = None
        for at in range(0, contacts, GROUP):
            cols = slice(at, at + GROUP)
            near_parts, far_parts = [], []
            for c in range(at, at + GROUP, LANES):
                spot = slice(c, c + LANES)
                near_parts.append(gather_columns(parts, lane1[:, spot], chunk1[:, spot]))
                far_parts.append(gather_columns(extended, lane2[:, spot], chunk2[:, spot]))
            u1 = jnp.concatenate(near_parts, axis=1)
            u2 = jnp.concatenate(far_parts, axis=1)
            w1 = w2 = None
            for r in range(6):
                a, b = g1[r, :, cols], g2[r, :, cols]
                strain = sum_rows(a * u1 + b * u2)
                w1 = a * strain if w1 is None else w1 + a * strain
                w2 = b * strain if w2 is None else w2 + b * strain
                if k == ITERS - 1:
                    energy = strain * strain if energy is None else energy + strain * strain
            put_first(left1, at, 0, w1, chunk1[:, cols] // 2, GROUP)
            put_second(left2, at, 0, w2, chunk2[:, cols] // 2, GROUP)
        if k == ITERS - 1:
            folded = energy[:, 0:LANES]
            for at in range(LANES, GROUP, LANES):
                folded = folded + energy[:, at : at + LANES]
            spring = sum_rows(dot_rows(v_now * prox8[...], v_now))
            moment[2 * k + 1 : 2 * k + 2, :] = (folded + spring)[0:1] - moment[2 * k : 2 * k + 1, :]
            part_copies = []
            for number, device in enumerate(part_near):
                part_copies.append(
                    pltpu.make_async_remote_copy(
                        src_ref=moment,
                        dst_ref=part_recv.at[number],
                        send_sem=part_ssem.at[number],
                        recv_sem=part_rsem.at[number],
                        device_id=device,
                        device_id_type=MESH,
                    )
                )
                part_copies[-1].start()
        product2 = one_hot_dot(left2[0:per_second], hot2[...])
        halo = halo_sum(product2, local_rows)
        back_send[k, 0] = halo[:, :LANES]
        back_send[k, 1] = halo[:, LANES:]
        copies = exchange(back_send.at[k], back_recv.at[k], back_ssem.at[k], back_rsem.at[k], forward)
        if k == ITERS - 1:
            settle(part_copies)
            total = moment[...]
            for number in range(len(part_near)):
                total = total + part_recv[number]
            whole_send[...] = total
            whole_copies = []
            for number, device in enumerate(whole_near):
                whole_copies.append(
                    pltpu.make_async_remote_copy(
                        src_ref=whole_send,
                        dst_ref=whole_recv.at[number],
                        send_sem=whole_ssem.at[number],
                        recv_sem=whole_rsem.at[number],
                        device_id=device,
                        device_id_type=MESH,
                    )
                )
                whole_copies[-1].start()
        product1 = one_hot_dot(left1[0:per_first], hot1[...])
        image = local_sum(product1, 0) + local_sum(product2, 0) + prox8[...] * v_now - q_now
        settle(copies)
        returned = arrange(lambda s: back_recv[k, s], reverse)
        put_first(leftb, 0, 0, returned, span_b, 2 * LANES)
        q_next = image + local_sum(one_hot_dot(leftb[0:per_first], hotb[...]), 0)
        basis_q[k + 1] = q_next
        if k < ITERS - 1:
            moment[2 * k + 1 : 2 * k + 2, :] = sum_rows(dot_rows(v_now, q_next))[0:1]
            basis_v[k + 1] = precondition(q_next)

    settle(whole_copies)
    total = whole_send[...]
    for number in range(len(whole_near)):
        total = total + whole_recv[number]
    sums = jnp.sum(total, axis=1, keepdims=True)
    moments = [jnp.broadcast_to(sums[i : i + 1, :], (ROWS, LANES)) for i in range(2 * ITERS)]
    along, left = coefficients(moments)
    for c in range(chunks):
        cols = slice(c * LANES, (c + 1) * LANES)
        value = along[0] * basis_v[0, :, cols]
        for j in range(1, ITERS):
            value = value + along[j] * basis_v[j, :, cols]
        step_ref[:, cols] = value[0:6]
        value = left[0] * basis_q[0, :, cols]
        for j in range(1, ITERS + 1):
            value = value + left[j] * basis_q[j, :, cols]
        residual_ref[:, cols] = value[0:6]


def local(mesh_shape, body_load, proximal, contact_blocks, slacks, dual_rows, first_body, second_body, border_bodies):
    nx, ny = mesh_shape
    ys = 4 if nx % 8 == 0 else 1
    zs = nx // (2 * ys)
    bodies, contacts = body_load.shape[3], contact_blocks.shape[4]
    spans = bodies // SPAN
    halves = SPLITS + SPLITS % 2
    first_rows, second_rows = ROWS * spans * SPLITS, ROWS * (spans * SPLITS + halves)
    f32, bf16, i32 = jnp.float32, jnp.bfloat16, jnp.int32
    vmem = pltpu.VMEM
    dma = pltpu.SemaphoreType.DMA
    parts, wholes = ny * ys - 1, 2 * zs - 1
    scratch = [
        vmem((6, ROWS, contacts), f32),
        vmem((6, ROWS, contacts), f32),
        vmem((SPAN, contacts), bf16),
        vmem((SPAN, contacts), bf16),
        vmem((SPAN, 2 * LANES), bf16),
        vmem((ROWS, contacts), i32),
        vmem((ROWS, contacts), i32),
        vmem((ROWS, contacts), i32),
        vmem((ROWS, contacts), i32),
        vmem((ROWS, 2 * LANES), i32),
        vmem((ROWS, 2 * LANES), i32),
        vmem((3 * first_rows, contacts), bf16),
        vmem((3 * second_rows, contacts), bf16),
        vmem((3 * first_rows, 2 * LANES), bf16),
        vmem((ITERS, ROWS, bodies), f32),
        vmem((ITERS + 1, ROWS, bodies), f32),
        vmem((ROWS, bodies), f32),
        vmem((6, ROWS, bodies), f32),
        vmem((3 * ROWS, bodies), f32),
        vmem((ROWS, LANES), i32),
        vmem((2, 3 * ROWS, LANES), f32),
        vmem((8, 3 * ROWS, LANES), f32),
        vmem((ITERS, 2, ROWS, LANES), f32),
        vmem((ITERS, 8, ROWS, LANES), f32),
        vmem((ITERS, 2, ROWS, LANES), f32),
        vmem((ITERS, 8, ROWS, LANES), f32),
        vmem((ROWS, LANES), f32),
        vmem((parts, ROWS, LANES), f32),
        vmem((ROWS, LANES), f32),
        vmem((wholes, ROWS, LANES), f32),
        dma((8,)),
        dma((8,)),
        dma((ITERS, 8)),
        dma((ITERS, 8)),
        dma((ITERS, 8)),
        dma((ITERS, 8)),
        dma((parts,)),
        dma((parts,)),
        dma((wholes,)),
        dma((wholes,)),
    ]
    step, residual = pl.pallas_call(
        functools.partial(kernel, (nx, ny, ys, zs)),
        out_shape=[jax.ShapeDtypeStruct((6, bodies), f32)] * 2,
        in_specs=[pl.BlockSpec(memory_space=pltpu.VMEM)] * 8,
        out_specs=[pl.BlockSpec(memory_space=pltpu.VMEM)] * 2,
        scratch_shapes=scratch,
        compiler_params=pltpu.CompilerParams(
            collective_id=0, has_side_effects=True, vmem_limit_bytes=48 * 1024 * 1024
        ),
    )(
        body_load[0, 0],
        proximal[0, 0],
        contact_blocks[0, 0],
        slacks[0, 0],
        dual_rows[0, 0],
        first_body[0],
        second_body[0],
        border_bodies[0, 0],
    )
    return step[None, None], residual[None, None]


def solution(mesh):
    return jax.shard_map(
        functools.partial(local, (mesh.shape["gx"], mesh.shape["gy"])),
        mesh=mesh,
        in_specs=(
            P("gx", "gy", None, None),
            P("gx", "gy", None, None),
            P("gx", "gy", None, None, None),
            P("gx", "gy", None, None),
            P("gx", "gy", None, None),
            P("gx", "gy", None),
            P("gx", "gy", None),
            P("gx", "gy", None, None),
        ),
        out_specs=(P("gx", "gy", None, None), P("gx", "gy", None, None)),
        check_vma=False,
    )
```

time: 1040 us -> 72.3 us (0.07); the launches traced: 1030 us -> 72.1 us
  blocking collectives: 558 us -> 0 us
  other arithmetic: 141 us -> 0 us
  matrix products: 99.3 us -> 0 us
  local copies, waits for them, and re-layouts: 98 us -> 4.13 us
  starting transfers between devices: 90.1 us -> 0 us
  Pallas kernels: 0 us -> 67.3 us
  waiting for transfers between devices: 26.7 us -> 0 us
  between operations: 12.4 us -> 0.7 us
    psum x7 -> x0, blocking collectives: 558 us -> none  [the longest x4 307 us: weighted_norm(): return lax.psum(jnp.sum(residual * preconditioned), ('gx', 'gy'))]
    scatter-add x15 -> x0, other arithmetic: 129 us -> none  [the longest x5 59.9 us: spread_ends(): extended = jnp.zeros((half_width, bodies + halo_slots), jnp.float32).at[:...]
    dot_general x5 -> x0, matrix products: 99.3 us -> none  [the longest x4 68.2 us: local(): values = jnp.einsum('ijc,jc->ic', stiffness, stacked, precision=HIGHEST)]
    ppermute x36 -> x0, starting transfers between devices: 90.1 us -> none  [the longest x18 61 us: with_halo(): before = lax.ppermute(last, axis, up)]
    pallas_call x0 -> x1, Pallas kernels: none -> 67.3 us  [local(): pl.pallas_call(functools.partial(kernel, (nx, ny, ys, zs)), out_shape=[ja...]
    gather x12 -> x0, local copies, waits for them, and re-layouts: 46.9 us -> none  [the longest x4 22.1 us: local(): jnp.take(extended, second_index, axis=1)]
    slice x49 -> x0, local copies, waits for them, and re-layouts: 26.8 us -> none  [the longest x2 21.1 us: local(): upper_blocks = stiffness[:6, :6].reshape(36, -1)]
    ppermute x36 -> x0, waiting for transfers between devices: 26.7 us -> none  [the longest x18 26.6 us: with_halo(): after = lax.ppermute(initial, axis, down)]
  transfers between devices with their start and end apart: 36 -> 0, of which waited for: 9 -> 0; matrix products, arithmetic and copies ran while one was open for 9% -> 0% of each run, Pallas kernels for 0% -> 0%
where the time goes in v1:
time: 72.3 us; the launch traced here: 72.1 us
  Pallas kernels  67.3 us (93%)
  local copies, waits for them, and re-layouts  4.13 us (6%)
    pallas_call x1, Pallas kernels, local(): pl.pallas_call(functools.partial(kernel, (nx, ny, ys, zs)), out_shape=[ja...  67.3 us
    unnamed x13, local copies, waits for them, and re-layouts  4.13 us

profile of v1, /device:TPU:1, one launch (start us, length us, event | category | flops | bytes accessed | tf_op | source)
XLA Modules:
  0.0 72.1 jit_solution(5494301648306553560)
XLA Ops:
  0.6 0.0 copy-start.3
  0.6 0.7 %copy_bitcast_fusion.3 = (f32[6,512]{1,0:T(8,128)S(1)}, f32[6,512]{1,0:T(8,128)S(1)}) fusion(f32[1,1,6,512]{3,1,2,0:T(1,128)} %param.9, f32[1,1,6,512]{3,1,2,0:T(1,128)} %param.8), kind=kLoop, calls=%fused_computation.3 | loop fusion | bytes 49152
  1.4 0.0 copy-done.3
  1.4 0.8 %copy_bitcast_fusion.1 = (f32[6,2048]{1,0:T(8,128)S(1)}, f32[6,2048]{1,0:T(8,128)S(1)}) fusion(f32[1,1,6,2048]{3,1,2,0:T(1,128)S(1)} %copy-done.3, f32[1,1,6,2048]{3,1,2,0:T(1,128)} %param.11), kind=kLoop, calls=%fused_computation.1 | loop fusion | bytes 196608
  2.3 0.0 copy-start
  2.3 0.0 copy-start.1
  2.3 0.0 copy-start.2
  2.3 1.3 %copy.22 = f32[1,1,6,12,2048]{4,3,1,2,0:T(8,128)S(1)} copy(f32[1,1,6,12,2048]{4,1,3,2,0:T(1,128)} %param.10) | data formatting | bytes 1179648
  3.6 0.0 copy-done
  3.6 0.0 copy-done.1
  3.6 0.0 copy-done.2
  3.6 67.3 %shard_map.95 = (f32[6,512]{1,0:T(8,128)S(1)}, f32[6,512]{1,0:T(8,128)S(1)}) custom-call(f32[6,512]{1,0:T(8,128)S(1)} %get-tuple-element.11.load_ref, f32[6,512]{1,0:T(8,128)S(1)} %get-tuple-element.10.prox_ref, f32[6,12,2048]{2,1,0:T(8,128)S(1)} %bitcast.16, f32[6,2048]{1,0:T(8,128)S(1)} %get-tuple-element.9.slack_ref, ...), custom_call_target="tpu_custom_call" | custom-call | tf_op jit(solution)/shard_map/pallas_call | solution.py:508
  70.9 0.6 copy.10
  71.5 0.6 copy.11
Async XLA Ops:
  0.6 0.8 %copy-start.3 = (f32[1,1,6,2048]{3,1,2,0:T(1,128)S(1)}, f32[1,1,6,2048]{3,1,2,0:T(1,128)}, u32[]{:S(2)}) copy-start(f32[1,1,6,2048]{3,1,2,0:T(1,128)} %param.12) | copy-start | bytes 147460
  2.3 1.3 %copy-start = (s32[1,1,2048]{2,1,0:T(1,128)S(1)}, s32[1,1,2048]{2,1,0:T(1,128)}, u32[]{:S(2)}) copy-start(s32[1,1,2048]{2,1,0:T(1,128)} %param.13) | copy-start | bytes 24580
  2.3 1.3 %copy-start.1 = (s32[1,1,2048]{2,1,0:T(1,128)S(1)}, s32[1,1,2048]{2,1,0:T(1,128)}, u32[]{:S(2)}) copy-start(s32[1,1,2048]{2,1,0:T(1,128)} %param.14) | copy-start | bytes 24580
  2.3 1.3 %copy-start.2 = (s32[1,1,8,32]{3,2,1,0:T(8,128)S(1)}, s32[1,1,8,32]{3,2,1,0:T(8,128)}, u32[]{:S(2)}) copy-start(s32[1,1,8,32]{3,2,1,0:T(8,128)} %param.15) | copy-start | bytes 3076

commit v2 on v0

v2 whole, which is shorter than its diff:
```python
import functools

import jax
import jax.numpy as jnp
from jax import lax
from jax.experimental import pallas as pl
from jax.experimental.pallas import tpu as pltpu
from jax.sharding import PartitionSpec as P

ITERS = 4
LANES = 128
ROWS = 8
SPAN = 256
SPLITS = 3
FIELDS = 6
PAIRS = [(a, b) for a in range(FIELDS) for b in range(a, FIELDS)]
PAIR_ROWS = 24
MESH = pl.DeviceIdType.MESH
OFFSETS = ((-1, -1), (-1, 0), (-1, 1), (0, -1), (0, 1), (1, -1), (1, 0), (1, 1))
SEND_ORDER = (0, 2, 5, 7, 1, 6, 3, 4)


def pick(source, lane):
    return jnp.take_along_axis(source, lane, axis=1, mode="promise_in_bounds")


def add_up(values):
    total = values[0]
    for value in values[1:]:
        total = total + value
    return total


def split_terms(values):
    terms = []
    for number in range(SPLITS):
        term = values.astype(jnp.bfloat16).astype(jnp.float32)
        terms.append(term)
        if number + 1 < SPLITS:
            values = values - term
    return terms


def dot(left, hot):
    return lax.dot_general(
        left, hot, (((1,), (0,)), ((), ())), preferred_element_type=jnp.float32
    )


def sum_rows(values):
    for shift in (4, 2, 1):
        values = values + pltpu.roll(values, shift, 0)
    return values


def inverse_six(entry):
    lower, flipped = {}, []
    for column in range(6):
        scaled = [lower[column, inner] * flipped[inner][0] for inner in range(column)]
        value = entry(column, column)
        for inner in range(column):
            value = value - scaled[inner] * lower[column, inner]
        flipped.append((value, 1.0 / value))
        for row in range(column + 1, 6):
            value = entry(column, row)
            for inner in range(column):
                value = value - lower[row, inner] * scaled[inner]
            lower[row, column] = value * flipped[column][1]
    unit = {}
    for column in range(6):
        for row in range(column + 1, 6):
            value = -lower[row, column]
            for inner in range(column + 1, row):
                value = value - lower[row, inner] * unit[inner, column]
            unit[row, column] = value
    result = {}
    for row in range(6):
        weighted = {inner: flipped[inner][1] * unit[inner, row] for inner in range(row + 1, 6)}
        weighted[row] = flipped[row][1]
        for column in range(row + 1):
            terms = []
            for inner in range(row, 6):
                term = weighted[inner]
                terms.append(term if inner == column else term * unit[inner, column])
            result[row, column] = result[column, row] = add_up(terms)
    return result


def coefficients(moments):
    def inner(left, right):
        weights = {}
        for i, a in enumerate(left):
            for j, b in enumerate(right):
                weights.setdefault(i + j, []).append(a * b)
        return add_up([add_up(w) * moments[i] for i, w in weights.items()])

    one = jnp.ones_like(moments[0])
    step = [None] * ITERS
    residual, direction = [one], [one]
    norm_now = moments[0]
    for iteration in range(ITERS):
        image = []
        for j in range(len(direction) + 1):
            image.append(add_up([direction[i] for i in (j - 1, j) if 0 <= i < len(direction)]))
        length = norm_now / inner(direction, image)
        for j, value in enumerate(direction):
            step[j] = length * value if step[j] is None else step[j] + length * value
        residual = [
            (residual[j] - length * image[j]) if j < len(residual) else -length * image[j]
            for j in range(len(image))
        ]
        if iteration + 1 < ITERS:
            norm_next = inner(residual, residual)
            ratio = norm_next / norm_now
            direction = [
                (residual[j] + ratio * direction[j]) if j < len(direction) else residual[j]
                for j in range(len(residual))
            ]
            norm_now = norm_next
    return step, residual


def kernel(
    sizes,
    load_hbm, prox_hbm, block_hbm, slack_hbm, dual_hbm, first_hbm, second_hbm, border_hbm,
    step_ref, residual_ref,
    load_in, prox_in, block_in, slack_in, dual_in, first_in, second_in, border_in, in_sem,
    g, hot1, hot2, hotb, span1, span2, spanb, laneb, chunkb, border_pad,
    left1, left2, left_halo, leftb, spread, spread_first, spread_pairs, spread_pairs_first,
    basis_v, basis_q, prox, inverse, diag, returned, columns,
    diag_send, diag_recv, fore_send, fore_recv, back_send, back_recv,
    part_send, part_recv, whole_send, whole_recv,
    diag_ssem, diag_rsem, fore_ssem, fore_rsem, back_ssem, back_rsem,
    part_ssem, part_rsem, whole_ssem, whole_rsem,
):
    nx, ny, ys, zs = sizes
    chunks = load_in.shape[0] // FIELDS
    spans = chunks * LANES // SPAN
    tiles = first_in.shape[0]
    f32, bf16 = jnp.float32, jnp.bfloat16
    gx, gy = lax.axis_index("gx"), lax.axis_index("gy")
    z_at, y_at, core = gx // (2 * ys), (gx // 2) % ys, gx % 2

    loads = []
    for number, (source, target) in enumerate(
        (
            (second_hbm, second_in),
            (block_hbm, block_in),
            (slack_hbm, slack_in),
            (dual_hbm, dual_in),
            (first_hbm, first_in),
            (border_hbm, border_in),
            (load_hbm, load_in),
            (prox_hbm, prox_in),
        )
    ):
        loads.append(pltpu.make_async_copy(source, target, in_sem.at[number]))
        loads[-1].start()

    near = [((gx + dx + nx) % nx, (gy + dy + ny) % ny) for dx, dy in OFFSETS]
    real = []
    for dx, dy in OFFSETS:
        to_x, to_y = gx + dx, gy + dy
        real.append((to_x >= 0) & (to_x < nx) & (to_y >= 0) & (to_y < ny))
    part_count, whole_count = ny * ys, zs * 2
    part_near, whole_near = [], []
    for offset in range(1, part_count):
        other = (gy * ys + y_at + offset) % part_count
        part_near.append((z_at * 2 * ys + (other % ys) * 2 + core, other // ys))
    for offset in range(1, whole_count):
        other = (z_at * 2 + core + offset) % whole_count
        whole_near.append(((other // 2) * 2 * ys + y_at * 2 + other % 2, gy))
    barrier = pltpu.get_barrier_semaphore()
    everyone = near + part_near + whole_near
    for device in everyone:
        pl.semaphore_signal(barrier, inc=1, device_id=device, device_id_type=MESH)

    lane_group = lax.broadcasted_iota(jnp.int32, (1, LANES), 1) // 32
    lane_at = lax.broadcasted_iota(jnp.int32, (LANES, LANES), 1)

    def build_hot(hot, row, at):
        spot = jnp.transpose(jnp.broadcast_to(row % SPAN, (LANES, LANES)).astype(f32))
        for part in range(SPAN // LANES):
            same = spot == (lane_at + part * LANES).astype(f32)
            hot[at : at + LANES, part * LANES : (part + 1) * LANES] = jnp.where(
                same, 1.0, 0.0
            ).astype(bf16)

    def write_terms(target, values, masks):
        pieces = [jnp.where(mask, t, 0.0) for t in split_terms(values) for mask in masks]
        if (len(pieces) * values.shape[1]) % 16:
            pieces.append(jnp.zeros((values.shape[0], ROWS, LANES), f32))
        packed = jnp.concatenate(pieces, axis=1).astype(bf16)
        for s in range(values.shape[0]):
            target[0 : packed.shape[1], s * LANES : (s + 1) * LANES] = packed[s]
        return packed.shape[1]

    def read_terms(product, rows, masks):
        result = []
        for mask in range(masks):
            total = add_up(
                [
                    product[(n * masks + mask) * rows : (n * masks + mask + 1) * rows]
                    for n in range(SPLITS)
                ]
            )
            result.extend([total[:, :LANES], total[:, LANES:]])
        return result

    def arrange(slots, place_of):
        halves = [[], []]
        for k in range(8):
            place = place_of(k)
            code = jnp.where(real[k], place % 4, -1)
            halves[place // 4].append(jnp.where(lane_group == code, slots(k), 0.0))
        return [add_up(half) for half in halves]

    def reverse(k):
        return 7 - k

    def forward(k):
        return k

    def exchange(send, recv, ssem, rsem, place_of):
        copies = []
        for k in SEND_ORDER:
            copies.append(
                pltpu.make_async_remote_copy(
                    src_ref=send.at[place_of(k) // 4],
                    dst_ref=recv.at[7 - k],
                    send_sem=ssem.at[k],
                    recv_sem=rsem.at[7 - k],
                    device_id=near[k],
                    device_id_type=MESH,
                )
            )
            copies[-1].start()
        return copies

    def broadcast_all(sender, receiver, ssem, rsem, devices):
        copies = []
        for number, device in enumerate(devices):
            copies.append(
                pltpu.make_async_remote_copy(
                    src_ref=sender,
                    dst_ref=receiver.at[number],
                    send_sem=ssem.at[number],
                    recv_sem=rsem.at[number],
                    device_id=device,
                    device_id_type=MESH,
                )
            )
            copies[-1].start()
        return copies

    def sent(copies):
        for copy in copies:
            copy.wait_send()

    def arrived(copies):
        for copy in copies:
            copy.wait_recv()

    spread[...] = jnp.zeros_like(spread)
    spread_first[...] = jnp.zeros_like(spread_first)
    spread_pairs[...] = jnp.zeros_like(spread_pairs)
    spread_pairs_first[...] = jnp.zeros_like(spread_pairs_first)
    loads[0].wait()
    for s in range(tiles):
        row = second_in[s : s + 1, :]
        span2[s] = jnp.broadcast_to(row // SPAN, (ROWS, LANES))
        build_hot(hot2, row, s * LANES)

    def masks_of(span, rows, wanted):
        value = span[...]
        if rows != ROWS:
            value = jnp.concatenate([value] * (rows // ROWS), axis=1)
        return [value == number for number in wanted]

    def pair_products(base, target):
        for p, (a, b) in enumerate(PAIRS):
            value = add_up([g[r * 12 + base + a] * g[r * 12 + base + b] for r in range(6)])
            target[pl.ds(p, tiles, stride=PAIR_ROWS), :] = value

    for number in (1, 2, 3):
        loads[number].wait()
    root = [jnp.sqrt(dual_in[r] / slack_in[r]) for r in range(6)]
    for r in range(6):
        for j in range(6, 12):
            g[r * 12 + j] = block_in[r * 12 + j] * root[r]
    pair_products(6, spread_pairs)
    pair_values = spread_pairs[...].reshape(tiles, PAIR_ROWS, LANES)
    rows = write_terms(left_halo, pair_values, masks_of(span2, PAIR_ROWS, [spans]))
    halves = read_terms(dot(left_halo[0:rows, :], hot2[...]), PAIR_ROWS, 1)
    for half in range(2):
        diag_send[half] = halves[half]
    pl.semaphore_wait(barrier, len(everyone))
    copies = exchange(diag_send, diag_recv, diag_ssem, diag_rsem, forward)

    rows = write_terms(left2, pair_values, masks_of(span2, PAIR_ROWS, range(spans)))
    local2 = read_terms(dot(left2[0:rows, :], hot2[...]), PAIR_ROWS, spans)
    for r in range(6):
        for j in range(6):
            g[r * 12 + j] = block_in[r * 12 + j] * root[r]
    pair_products(0, spread_pairs_first)
    loads[4].wait()
    for s in range(tiles):
        row = first_in[s : s + 1, :]
        span1[s] = jnp.broadcast_to(row // SPAN, (ROWS, LANES))
        build_hot(hot1, row, s * LANES)
    pair_values = spread_pairs_first[...].reshape(tiles, PAIR_ROWS, LANES)
    rows = write_terms(left1, pair_values, masks_of(span1, PAIR_ROWS, range(spans)))
    local1 = read_terms(dot(left1[0:rows, :], hot1[...]), PAIR_ROWS, spans)
    for c in range(chunks):
        diag[c] = local1[c] + local2[c]
    loads[5].wait()
    border_pad[...] = jnp.zeros_like(border_pad)
    border_pad[:, : border_in.shape[1]] = border_in[...]
    for half in range(2):
        row = border_pad[7 - 4 * half : 8 - 4 * half, :]
        for quarter in range(1, 4):
            place = 4 * half + quarter
            moved = pltpu.roll(border_pad[7 - place : 8 - place, :], 32 * quarter, 1)
            row = jnp.where(lane_group == quarter, moved, row)
        build_hot(hotb, row, half * LANES)
        whole = jnp.broadcast_to(row, (ROWS, LANES))
        laneb[half] = whole % LANES
        chunkb[half] = whole // LANES
        spanb[half] = whole // SPAN
    loads[6].wait()
    loads[7].wait()
    zero_rows = jnp.zeros((ROWS - FIELDS, LANES), f32)
    for c in range(chunks):
        basis_q[0, c] = jnp.concatenate(
            [load_in[pl.ds(c, FIELDS, stride=chunks), :], zero_rows], axis=0
        )
        prox[c] = jnp.concatenate(
            [prox_in[pl.ds(c, FIELDS, stride=chunks), :], zero_rows], axis=0
        )
    inverse[...] = jnp.zeros_like(inverse)
    columns[...] = jnp.zeros_like(columns)
    lane1, chunk1 = first_in[...] % LANES, first_in[...] // LANES
    lane2, chunk2 = second_in[...] % LANES, second_in[...] // LANES

    sent(copies)
    arrived(copies)
    halves = arrange(lambda k: diag_recv[k], reverse)
    for half in range(2):
        returned[half] = halves[half]
    rows = write_terms(leftb, returned[...], masks_of(spanb, PAIR_ROWS, range(spans)))
    localb = read_terms(dot(leftb[0:rows, :], hotb[...]), PAIR_ROWS, spans)
    entries = {}
    for c in range(chunks):
        spread_pairs[pl.ds(c, PAIR_ROWS, stride=ROWS), :] = diag[c] + localb[c]
    for p, (a, b) in enumerate(PAIRS):
        value = spread_pairs[p * ROWS : p * ROWS + chunks, :]
        if a == b:
            value = value + prox_in[a * chunks : (a + 1) * chunks, :]
        entries[a, b] = value
    for (a, b), value in inverse_six(lambda a, b: entries[a, b]).items():
        inverse[pl.ds(b * chunks * ROWS + a, chunks, stride=ROWS), :] = value

    def precondition(field):
        result = []
        for c in range(chunks):
            terms = []
            for b in range(FIELDS):
                at = (b * chunks + c) * ROWS
                terms.append(
                    inverse[at : at + ROWS, :]
                    * jnp.broadcast_to(field[c][b : b + 1, :], (ROWS, LANES))
                )
            result.append(add_up(terms))
        return result

    moments = jnp.zeros((1, LANES), f32)
    moment_group = lax.broadcasted_iota(jnp.int32, (1, LANES), 1) // 16

    def fold(value):
        value = sum_rows(value)[0:1]
        for shift in (64, 32, 16):
            value = value + pltpu.roll(value, shift, 1)
        return value

    def inner(left, right):
        return fold(add_up([left[c] * right[c] for c in range(chunks)]))

    def gather_fields(rows_of, lane, chunk, start, count):
        result = []
        for f in range(FIELDS):
            value = None
            for n in range(count):
                source = jnp.broadcast_to(rows_of(f, n), (tiles, LANES))
                piece = pick(source, lane)
                if value is None:
                    value = piece if start == 0 else jnp.where(chunk == start, piece, 0.0)
                else:
                    value = jnp.where(chunk == start + n, piece, value)
            result.append(value)
        return result

    q_now = [basis_q[0, c] for c in range(chunks)]
    v_now = precondition(q_now)
    late = []
    for k in range(ITERS):
        for c in range(chunks):
            basis_v[k, c] = v_now[c]
        ends = []
        for half in range(2):
            value = pick(v_now[0], laneb[half])
            for c in range(1, chunks):
                value = jnp.where(chunkb[half] == c, pick(v_now[c], laneb[half]), value)
            ends.append(value)
            fore_send[k, half] = value
        fore = exchange(
            fore_send.at[k], fore_recv.at[k], fore_ssem.at[k], fore_rsem.at[k], reverse
        )
        u1 = gather_fields(lambda f, n: basis_v[k, n, f : f + 1, :], lane1, chunk1, 0, chunks)
        u2 = gather_fields(lambda f, n: basis_v[k, n, f : f + 1, :], lane2, chunk2, 0, chunks)
        here = chunk2 < chunks
        u2 = [jnp.where(here, value, 0.0) for value in u2]
        strain = []
        for r in range(6):
            strain.append(
                add_up(
                    [g[r * 12 + j] * u1[j] for j in range(6)]
                    + [g[r * 12 + 6 + j] * u2[j] for j in range(6)]
                )
            )
        for j in range(6):
            value = add_up([g[r * 12 + 6 + j] * strain[r] for r in range(6)])
            spread[pl.ds(j, tiles, stride=ROWS), :] = value
        pulls = spread[...].reshape(tiles, ROWS, LANES)
        rows = write_terms(left_halo, pulls, masks_of(span2, ROWS, [spans]))
        halves = read_terms(dot(left_halo[0:rows, :], hot2[...]), ROWS, 1)
        for half in range(2):
            back_send[k, half] = halves[half]
        back = exchange(
            back_send.at[k], back_recv.at[k], back_ssem.at[k], back_rsem.at[k], forward
        )
        rows = write_terms(left2, pulls, masks_of(span2, ROWS, range(spans)))
        image = read_terms(dot(left2[0:rows, :], hot2[...]), ROWS, spans)
        image = [image[c] + prox[c] * v_now[c] - q_now[c] for c in range(chunks)]
        pushes = [add_up([g[r * 12 + j] * strain[r] for r in range(6)]) for j in range(6)]
        if k == 0:
            for p, (a, b) in enumerate(PAIRS):
                for half in range(2):
                    row = returned[half, p : p + 1, :]
                    columns[b, half, a : a + 1, :] = row
                    if a != b:
                        columns[a, half, b : b + 1, :] = row
        pulled = []
        for half in range(2):
            pulled.append(
                add_up(
                    [
                        columns[b, half]
                        * jnp.broadcast_to(ends[half][b : b + 1, :], (ROWS, LANES))
                        for b in range(FIELDS)
                    ]
                )
            )
        norm = inner(v_now, q_now)
        moments = jnp.where(moment_group == 2 * k, norm, moments)
        sent(late)
        sent(fore)
        arrived(fore)
        beyond = arrange(lambda s: fore_recv[k, s], forward)
        u2 = gather_fields(lambda f, n: beyond[n][f : f + 1, :], lane2, chunk2, chunks, 2)
        more = [
            add_up([g[r * 12 + 6 + j] * u2[j] for j in range(6)]) for r in range(6)
        ]
        for j in range(6):
            value = pushes[j] + add_up([g[r * 12 + j] * more[r] for r in range(6)])
            spread_first[pl.ds(j, tiles, stride=ROWS), :] = value
        if k == ITERS - 1:
            energy = add_up([(strain[r] + more[r]) * (strain[r] + more[r]) for r in range(6)])
            energy = add_up([energy[t : t + ROWS] for t in range(0, tiles, ROWS)])
            energy = energy + add_up([prox[c] * v_now[c] * v_now[c] for c in range(chunks)])
            last = fold(energy) - norm
            part_send[...] = jnp.where(moment_group == 2 * k + 1, last, moments)
            part = broadcast_all(part_send, part_recv, part_ssem, part_rsem, part_near)
        values = spread_first[...].reshape(tiles, ROWS, LANES)
        rows = write_terms(left1, values, masks_of(span1, ROWS, range(spans)))
        pushed = read_terms(dot(left1[0:rows, :], hot1[...]), ROWS, spans)
        image = [image[c] + pushed[c] for c in range(chunks)]
        arrived(back)
        late = back
        halves = arrange(lambda s: back_recv[k, s], reverse)
        values = jnp.concatenate([(halves[h] + pulled[h])[None] for h in range(2)], axis=0)
        rows = write_terms(leftb, values, masks_of(spanb, ROWS, range(spans)))
        added = read_terms(dot(leftb[0:rows, :], hotb[...]), ROWS, spans)
        q_next = [image[c] + added[c] for c in range(chunks)]
        for c in range(chunks):
            basis_q[k + 1, c] = q_next[c]
        if k < ITERS - 1:
            v_next = precondition(q_next)
            moments = jnp.where(moment_group == 2 * k + 1, inner(v_now, q_next), moments)
            q_now, v_now = q_next, v_next

    sent(late)
    sent(part)
    arrived(part)
    whole_send[...] = part_send[...] + add_up([part_recv[n] for n in range(len(part_near))])
    copies = broadcast_all(whole_send, whole_recv, whole_ssem, whole_rsem, whole_near)
    sent(copies)
    arrived(copies)
    total = whole_send[...] + add_up([whole_recv[n] for n in range(len(whole_near))])
    row_at = lax.broadcasted_iota(jnp.int32, (ROWS, LANES), 0)
    group_at = lax.broadcasted_iota(jnp.int32, (ROWS, LANES), 1) // 16
    total = jnp.where(row_at == group_at, jnp.broadcast_to(total, (ROWS, LANES)), 0.0)
    sums = jnp.sum(total, axis=1, keepdims=True)
    along, left = coefficients(
        [jnp.broadcast_to(sums[i : i + 1, :], (ROWS, LANES)) for i in range(2 * ITERS)]
    )
    for c in range(chunks):
        value = add_up([along[j] * basis_v[j, c] for j in range(ITERS)])
        step_ref[pl.ds(c, FIELDS, stride=chunks), :] = value[0:FIELDS]
        value = add_up([left[j] * basis_q[j, c] for j in range(ITERS + 1)])
        residual_ref[pl.ds(c, FIELDS, stride=chunks), :] = value[0:FIELDS]


def local(mesh_shape, body_load, proximal, contact_blocks, slacks, dual_rows, first_body, second_body, border_bodies):
    nx, ny = mesh_shape
    ys = 4 if nx % 8 == 0 else 1
    zs = nx // (2 * ys)
    bodies, contacts = body_load.shape[3], contact_blocks.shape[4]
    chunks, tiles, spans = bodies // LANES, contacts // LANES, bodies // SPAN
    f32, bf16, i32 = jnp.float32, jnp.bfloat16, jnp.int32
    vmem = pltpu.VMEM
    dma = pltpu.SemaphoreType.DMA
    parts, wholes = ny * ys - 1, 2 * zs - 1
    pair_rows = PAIR_ROWS * SPLITS
    operands = (
        body_load.reshape(FIELDS * chunks, LANES),
        proximal.reshape(FIELDS * chunks, LANES),
        contact_blocks.reshape(12 * FIELDS, tiles, LANES),
        slacks.reshape(FIELDS, tiles, LANES),
        dual_rows.reshape(FIELDS, tiles, LANES),
        first_body.reshape(tiles, LANES),
        second_body.reshape(tiles, LANES),
        border_bodies.reshape(border_bodies.shape[2:]),
    )
    scratch = [vmem(a.shape, a.dtype) for a in operands] + [
        dma((8,)),
        vmem((12 * FIELDS, tiles, LANES), f32),
        vmem((contacts, SPAN), bf16),
        vmem((contacts, SPAN), bf16),
        vmem((2 * LANES, SPAN), bf16),
        vmem((tiles, ROWS, LANES), i32),
        vmem((tiles, ROWS, LANES), i32),
        vmem((2, ROWS, LANES), i32),
        vmem((2, ROWS, LANES), i32),
        vmem((2, ROWS, LANES), i32),
        vmem((ROWS, LANES), i32),
        vmem((pair_rows * spans, contacts), bf16),
        vmem((pair_rows * spans, contacts), bf16),
        vmem((pair_rows + ROWS, contacts), bf16),
        vmem((pair_rows * spans, 2 * LANES), bf16),
        vmem((tiles * ROWS, LANES), f32),
        vmem((tiles * ROWS, LANES), f32),
        vmem((tiles * PAIR_ROWS, LANES), f32),
        vmem((tiles * PAIR_ROWS, LANES), f32),
        vmem((ITERS, chunks, ROWS, LANES), f32),
        vmem((ITERS + 1, chunks, ROWS, LANES), f32),
        vmem((chunks, ROWS, LANES), f32),
        vmem((FIELDS * chunks * ROWS, LANES), f32),
        vmem((chunks, PAIR_ROWS, LANES), f32),
        vmem((2, PAIR_ROWS, LANES), f32),
        vmem((FIELDS, 2, ROWS, LANES), f32),
        vmem((2, PAIR_ROWS, LANES), f32),
        vmem((8, PAIR_ROWS, LANES), f32),
        vmem((ITERS, 2, ROWS, LANES), f32),
        vmem((ITERS, 8, ROWS, LANES), f32),
        vmem((ITERS, 2, ROWS, LANES), f32),
        vmem((ITERS, 8, ROWS, LANES), f32),
        vmem((1, LANES), f32),
        vmem((parts, 1, LANES), f32),
        vmem((1, LANES), f32),
        vmem((wholes, 1, LANES), f32),
        dma((8,)),
        dma((8,)),
        dma((ITERS, 8)),
        dma((ITERS, 8)),
        dma((ITERS, 8)),
        dma((ITERS, 8)),
        dma((parts,)),
        dma((parts,)),
        dma((wholes,)),
        dma((wholes,)),
    ]
    step, residual = pl.pallas_call(
        functools.partial(kernel, (nx, ny, ys, zs)),
        out_shape=[jax.ShapeDtypeStruct((FIELDS * chunks, LANES), f32)] * 2,
        in_specs=[pl.BlockSpec(memory_space=pl.ANY)] * 8,
        out_specs=[pl.BlockSpec(memory_space=pltpu.VMEM)] * 2,
        scratch_shapes=scratch,
        compiler_params=pltpu.CompilerParams(
            collective_id=0, has_side_effects=True, vmem_limit_bytes=56 * 1024 * 1024
        ),
    )(*operands)
    return step.reshape(body_load.shape), residual.reshape(body_load.shape)


def solution(mesh):
    return jax.shard_map(
        functools.partial(local, (mesh.shape["gx"], mesh.shape["gy"])),
        mesh=mesh,
        in_specs=(
            P("gx", "gy", None, None),
            P("gx", "gy", None, None),
            P("gx", "gy", None, None, None),
            P("gx", "gy", None, None),
            P("gx", "gy", None, None),
            P("gx", "gy", None),
            P("gx", "gy", None),
            P("gx", "gy", None, None),
        ),
        out_specs=(P("gx", "gy", None, None), P("gx", "gy", None, None)),
        check_vma=False,
    )
```

time: 1040 us -> 51.9 us (0.05); the launches traced: 1030 us -> 51.8 us
  blocking collectives: 558 us -> 0 us
  other arithmetic: 141 us -> 0 us
  matrix products: 99.3 us -> 0 us
  local copies, waits for them, and re-layouts: 98 us -> 1.92 us
  starting transfers between devices: 90.1 us -> 0 us
  Pallas kernels: 0 us -> 49.2 us
  waiting for transfers between devices: 26.7 us -> 0 us
  between operations: 12.4 us -> 0.65 us
    psum x7 -> x0, blocking collectives: 558 us -> none  [the longest x4 307 us: weighted_norm(): return lax.psum(jnp.sum(residual * preconditioned), ('gx', 'gy'))]
    scatter-add x15 -> x0, other arithmetic: 129 us -> none  [the longest x5 59.9 us: spread_ends(): extended = jnp.zeros((half_width, bodies + halo_slots), jnp.float32).at[:...]
    dot_general x5 -> x0, matrix products: 99.3 us -> none  [the longest x4 68.2 us: local(): values = jnp.einsum('ijc,jc->ic', stiffness, stacked, precision=HIGHEST)]
    ppermute x36 -> x0, starting transfers between devices: 90.1 us -> none  [the longest x18 61 us: with_halo(): before = lax.ppermute(last, axis, up)]
    pallas_call x0 -> x1, Pallas kernels: none -> 49.2 us  [local(): pl.pallas_call(functools.partial(kernel, (nx, ny, ys, zs)), out_shape=[ja...]
    gather x12 -> x0, local copies, waits for them, and re-layouts: 46.9 us -> none  [the longest x4 22.1 us: local(): jnp.take(extended, second_index, axis=1)]
    slice x49 -> x0, local copies, waits for them, and re-layouts: 26.8 us -> none  [the longest x2 21.1 us: local(): upper_blocks = stiffness[:6, :6].reshape(36, -1)]
    ppermute x36 -> x0, waiting for transfers between devices: 26.7 us -> none  [the longest x18 26.6 us: with_halo(): after = lax.ppermute(initial, axis, down)]
  transfers between devices with their start and end apart: 36 -> 0, of which waited for: 9 -> 0; matrix products, arithmetic and copies ran while one was open for 9% -> 0% of each run, Pallas kernels for 0% -> 0%
where the time goes in v2:
time: 51.9 us; the launch traced here: 51.8 us
  Pallas kernels  49.2 us (95%)
  local copies, waits for them, and re-layouts  1.92 us (4%)
  between operations  0.65 us (1%)
    pallas_call x1, Pallas kernels, local(): pl.pallas_call(functools.partial(kernel, (nx, ny, ys, zs)), out_shape=[ja...  49.2 us
    unnamed x4, local copies, waits for them, and re-layouts  1.92 us

profile of v2, /device:TPU:1, one launch (start us, length us, event | category | flops | bytes accessed | tf_op | source)
XLA Modules:
  0.0 51.8 jit_solution(11509251353580843752)
XLA Ops:
  0.6 49.2 %shard_map.95 = (f32[24,128]{1,0:T(8,128)}, f32[24,128]{1,0:T(8,128)}) custom-call(f32[24,128]{1,0:T(8,128)} %bitcast.15, f32[24,128]{1,0:T(8,128)} %bitcast.16, f32[72,16,128]{2,1,0:T(8,128)} %bitcast.10, f32[6,16,128]{2,1,0:T(8,128)} %bitcast.11, f32[6,16,128]{2,1,0:T(8,128)} %bitcast.12, s32[16,128]{1,0:T(8,128)} %bitcast.17, s32[16,128]{1,0:T(8,128)} %bitcast.18, ...), custom_call_target="tpu_custom_call" | custom-call | tf_op jit(solution)/shard_map/pallas_call | solution.py:592
  49.9 0.0 copy-start
  49.9 1.3 %copy.16 = f32[1,1,6,512]{3,1,2,0:T(1,128)} copy(f32[1,1,6,512]{3,1,2,0:T(1,128)} %bitcast.14) | data formatting | bytes 24576
  51.2 0.0 copy-done
  51.2 0.6 %copy.17 = f32[1,1,6,512]{3,1,2,0:T(1,128)} copy(f32[1,1,6,512]{3,1,2,0:T(1,128)S(1)} %bitcast.13) | data formatting | bytes 24576
Async XLA Ops:
  49.9 1.3 %copy-start = (f32[24,128]{1,0:T(8,128)S(1)}, f32[24,128]{1,0:T(8,128)}, u32[]{:S(2)}) copy-start(f32[24,128]{1,0:T(8,128)} %get-tuple-element.5) | copy-start | bytes 36868

commit v3 on v2

--- a/solution.py
+++ b/solution.py
@@ -17,7 +17,8 @@
 PAIR_ROWS = 24
 MESH = pl.DeviceIdType.MESH
 OFFSETS = ((-1, -1), (-1, 0), (-1, 1), (0, -1), (0, 1), (1, -1), (1, 0), (1, 1))
-SEND_ORDER = (0, 2, 5, 7, 1, 6, 3, 4)
+FAR = (0, 2, 5, 7)
+CLOSE = (1, 6, 3, 4)
 
 
 def pick(source, lane):
@@ -86,38 +87,42 @@
     return result
 
 
+def weigh(left, right, moments, skip=None):
+    weights = {}
+    for i, a in enumerate(left):
+        for j, b in enumerate(right):
+            if i + j != skip:
+                weights.setdefault(i + j, []).append(a * b)
+    return add_up([add_up(w) * moments[i] for i, w in weights.items()])
+
+
+def image_of(direction):
+    return [
+        add_up([direction[i] for i in (j - 1, j) if 0 <= i < len(direction)])
+        for j in range(len(direction) + 1)
+    ]
+
+
 def coefficients(moments):
-    def inner(left, right):
-        weights = {}
-        for i, a in enumerate(left):
-            for j, b in enumerate(right):
-                weights.setdefault(i + j, []).append(a * b)
-        return add_up([add_up(w) * moments[i] for i, w in weights.items()])
-
     one = jnp.ones_like(moments[0])
-    step = [None] * ITERS
-    residual, direction = [one], [one]
+    step, residual, direction = [], [one], [one]
     norm_now = moments[0]
-    for iteration in range(ITERS):
-        image = []
-        for j in range(len(direction) + 1):
-            image.append(add_up([direction[i] for i in (j - 1, j) if 0 <= i < len(direction)]))
-        length = norm_now / inner(direction, image)
-        for j, value in enumerate(direction):
-            step[j] = length * value if step[j] is None else step[j] + length * value
-        residual = [
-            (residual[j] - length * image[j]) if j < len(residual) else -length * image[j]
-            for j in range(len(image))
-        ]
-        if iteration + 1 < ITERS:
-            norm_next = inner(residual, residual)
-            ratio = norm_next / norm_now
-            direction = [
-                (residual[j] + ratio * direction[j]) if j < len(direction) else residual[j]
-                for j in range(len(residual))
-            ]
-            norm_now = norm_next
-    return step, residual
+    for iteration in range(ITERS - 1):
+        image = image_of(direction)
+        length = norm_now / weigh(direction, image, moments)
+        step = [a + length * b for a, b in zip(step, direction)] + [length * direction[-1]]
+        residual = [a - length * b for a, b in zip(residual, image)] + [-length * image[-1]]
+        norm_next = weigh(residual, residual, moments)
+        ratio = norm_next / norm_now
+        direction = [a + ratio * b for a, b in zip(residual, direction)] + [residual[-1]]
+        norm_now = norm_next
+    return step, residual, direction, image_of(direction), norm_now
+
+
+def energy_rest(direction, image, moments):
+    top = len(direction) - 1
+    rest = weigh(direction, image, moments, skip=2 * top + 1)
+    return rest - direction[top] * image[top + 1] * moments[2 * top]
 
 
 def kernel(
@@ -129,8 +134,10 @@
     left1, left2, left_halo, leftb, spread, spread_first, spread_pairs, spread_pairs_first,
     basis_v, basis_q, prox, inverse, diag, returned, columns,
     diag_send, diag_recv, fore_send, fore_recv, back_send, back_recv,
+    early_send, early_recv, early_whole_send, early_whole_recv,
     part_send, part_recv, whole_send, whole_recv,
     diag_ssem, diag_rsem, fore_ssem, fore_rsem, back_ssem, back_rsem,
+    early_ssem, early_rsem, early_whole_ssem, early_whole_rsem,
     part_ssem, part_rsem, whole_ssem, whole_rsem,
 ):
     nx, ny, ys, zs = sizes
@@ -140,6 +147,24 @@
     f32, bf16 = jnp.float32, jnp.bfloat16
     gx, gy = lax.axis_index("gx"), lax.axis_index("gy")
     z_at, y_at, core = gx // (2 * ys), (gx // 2) % ys, gx % 2
+
+    near = [((gx + dx + nx) % nx, (gy + dy + ny) % ny) for dx, dy in OFFSETS]
+    real = []
+    for dx, dy in OFFSETS:
+        to_x, to_y = gx + dx, gy + dy
+        real.append((to_x >= 0) & (to_x < nx) & (to_y >= 0) & (to_y < ny))
+    part_count, whole_count = ny * ys, zs * 2
+    part_near, whole_near = [], []
+    for offset in range(part_count):
+        other = (gy * ys + y_at + offset) % part_count
+        part_near.append((z_at * 2 * ys + (other % ys) * 2 + 1 - core, other // ys))
+    for offset in range(1, whole_count):
+        other = (z_at * 2 + core + offset) % whole_count
+        whole_near.append(((other // 2) * 2 * ys + y_at * 2 + other % 2, gy))
+    barrier = pltpu.get_barrier_semaphore()
+    everyone = [near[k] for k in FAR + CLOSE] + part_near + whole_near
+    for device in everyone:
+        pl.semaphore_signal(barrier, inc=1, device_id=device, device_id_type=MESH)
 
     loads = []
     for number, (source, target) in enumerate(
@@ -157,24 +182,6 @@
         loads.append(pltpu.make_async_copy(source, target, in_sem.at[number]))
         loads[-1].start()
 
-    near = [((gx + dx + nx) % nx, (gy + dy + ny) % ny) for dx, dy in OFFSETS]
-    real = []
-    for dx, dy in OFFSETS:
-        to_x, to_y = gx + dx, gy + dy
-        real.append((to_x >= 0) & (to_x < nx) & (to_y >= 0) & (to_y < ny))
-    part_count, whole_count = ny * ys, zs * 2
-    part_near, whole_near = [], []
-    for offset in range(1, part_count):
-        other = (gy * ys + y_at + offset) % part_count
-        part_near.append((z_at * 2 * ys + (other % ys) * 2 + core, other // ys))
-    for offset in range(1, whole_count):
-        other = (z_at * 2 + core + offset) % whole_count
-        whole_near.append(((other // 2) * 2 * ys + y_at * 2 + other % 2, gy))
-    barrier = pltpu.get_barrier_semaphore()
-    everyone = near + part_near + whole_near
-    for device in everyone:
-        pl.semaphore_signal(barrier, inc=1, device_id=device, device_id_type=MESH)
-
     lane_group = lax.broadcasted_iota(jnp.int32, (1, LANES), 1) // 32
     lane_at = lax.broadcasted_iota(jnp.int32, (LANES, LANES), 1)
 
@@ -221,9 +228,9 @@
     def forward(k):
         return k
 
-    def exchange(send, recv, ssem, rsem, place_of):
+    def exchange(send, recv, ssem, rsem, place_of, directions=FAR + CLOSE):
         copies = []
-        for k in SEND_ORDER:
+        for k in directions:
             copies.append(
                 pltpu.make_async_remote_copy(
                     src_ref=send.at[place_of(k) // 4],
@@ -376,14 +383,11 @@
     moments = jnp.zeros((1, LANES), f32)
     moment_group = lax.broadcasted_iota(jnp.int32, (1, LANES), 1) // 16
 
-    def fold(value):
-        value = sum_rows(value)[0:1]
+    def inner(left, right):
+        value = sum_rows(add_up([left[c] * right[c] for c in range(chunks)]))[0:1]
         for shift in (64, 32, 16):
             value = value + pltpu.roll(value, shift, 1)
         return value
-
-    def inner(left, right):
-        return fold(add_up([left[c] * right[c] for c in range(chunks)]))
 
     def gather_fields(rows_of, lane, chunk, start, count):
         result = []
@@ -412,21 +416,11 @@
                 value = jnp.where(chunkb[half] == c, pick(v_now[c], laneb[half]), value)
             ends.append(value)
             fore_send[k, half] = value
-        fore = exchange(
-            fore_send.at[k], fore_recv.at[k], fore_ssem.at[k], fore_rsem.at[k], reverse
-        )
+        fore_refs = (fore_send.at[k], fore_recv.at[k], fore_ssem.at[k], fore_rsem.at[k], reverse)
+        back_refs = (back_send.at[k], back_recv.at[k], back_ssem.at[k], back_rsem.at[k], forward)
+        fore = exchange(*fore_refs, FAR)
         u1 = gather_fields(lambda f, n: basis_v[k, n, f : f + 1, :], lane1, chunk1, 0, chunks)
-        u2 = gather_fields(lambda f, n: basis_v[k, n, f : f + 1, :], lane2, chunk2, 0, chunks)
-        here = chunk2 < chunks
-        u2 = [jnp.where(here, value, 0.0) for value in u2]
-        strain = []
-        for r in range(6):
-            strain.append(
-                add_up(
-                    [g[r * 12 + j] * u1[j] for j in range(6)]
-                    + [g[r * 12 + 6 + j] * u2[j] for j in range(6)]
-                )
-            )
+        strain = [add_up([g[r * 12 + j] * u1[j] for j in range(6)]) for r in range(6)]
         for j in range(6):
             value = add_up([g[r * 12 + 6 + j] * strain[r] for r in range(6)])
             spread[pl.ds(j, tiles, stride=ROWS), :] = value
@@ -435,9 +429,24 @@
         halves = read_terms(dot(left_halo[0:rows, :], hot2[...]), ROWS, 1)
         for half in range(2):
             back_send[k, half] = halves[half]
-        back = exchange(
-            back_send.at[k], back_recv.at[k], back_ssem.at[k], back_rsem.at[k], forward
-        )
+        back = exchange(*back_refs, FAR)
+        fore = fore + exchange(*fore_refs, CLOSE)
+        back = back + exchange(*back_refs, CLOSE)
+        norm = inner(v_now, q_now)
+        moments = jnp.where(moment_group == 2 * k, norm, moments)
+        if k == ITERS - 1:
+            early_send[...] = moments
+            early = broadcast_all(early_send, early_recv, early_ssem, early_rsem, part_near)
+        u2 = gather_fields(lambda f, n: basis_v[k, n, f : f + 1, :], lane2, chunk2, 0, chunks)
+        here = chunk2 < chunks
+        u2 = [jnp.where(here, value, 0.0) for value in u2]
+        strain = [
+            strain[r] + add_up([g[r * 12 + 6 + j] * u2[j] for j in range(6)]) for r in range(6)
+        ]
+        for j in range(6):
+            value = add_up([g[r * 12 + 6 + j] * strain[r] for r in range(6)])
+            spread[pl.ds(j, tiles, stride=ROWS), :] = value
+        pulls = spread[...].reshape(tiles, ROWS, LANES)
         rows = write_terms(left2, pulls, masks_of(span2, ROWS, range(spans)))
         image = read_terms(dot(left2[0:rows, :], hot2[...]), ROWS, spans)
         image = [image[c] + prox[c] * v_now[c] - q_now[c] for c in range(chunks)]
@@ -460,8 +469,6 @@
                     ]
                 )
             )
-        norm = inner(v_now, q_now)
-        moments = jnp.where(moment_group == 2 * k, norm, moments)
         sent(late)
         sent(fore)
         arrived(fore)
@@ -477,8 +484,7 @@
             energy = add_up([(strain[r] + more[r]) * (strain[r] + more[r]) for r in range(6)])
             energy = add_up([energy[t : t + ROWS] for t in range(0, tiles, ROWS)])
             energy = energy + add_up([prox[c] * v_now[c] * v_now[c] for c in range(chunks)])
-            last = fold(energy) - norm
-            part_send[...] = jnp.where(moment_group == 2 * k + 1, last, moments)
+            part_send[...] = sum_rows(energy)[0:1]
             part = broadcast_all(part_send, part_recv, part_ssem, part_rsem, part_near)
         values = spread_first[...].reshape(tiles, ROWS, LANES)
         rows = write_terms(left1, values, masks_of(span1, ROWS, range(spans)))
@@ -498,26 +504,44 @@
             moments = jnp.where(moment_group == 2 * k + 1, inner(v_now, q_next), moments)
             q_now, v_now = q_next, v_next
 
+    sent(early)
+    arrived(early)
+    early_whole_send[...] = add_up([early_recv[n] for n in range(len(part_near))])
+    early = broadcast_all(
+        early_whole_send, early_whole_recv, early_whole_ssem, early_whole_rsem, whole_near
+    )
     sent(late)
     sent(part)
     arrived(part)
-    whole_send[...] = part_send[...] + add_up([part_recv[n] for n in range(len(part_near))])
-    copies = broadcast_all(whole_send, whole_recv, whole_ssem, whole_rsem, whole_near)
-    sent(copies)
-    arrived(copies)
-    total = whole_send[...] + add_up([whole_recv[n] for n in range(len(whole_near))])
+    whole_send[...] = add_up([part_recv[n] for n in range(len(part_near))])
+    whole = broadcast_all(whole_send, whole_recv, whole_ssem, whole_rsem, whole_near)
+    sent(early)
+    arrived(early)
+    total = early_whole_send[...] + add_up([early_whole_recv[n] for n in range(len(whole_near))])
     row_at = lax.broadcasted_iota(jnp.int32, (ROWS, LANES), 0)
     group_at = lax.broadcasted_iota(jnp.int32, (ROWS, LANES), 1) // 16
     total = jnp.where(row_at == group_at, jnp.broadcast_to(total, (ROWS, LANES)), 0.0)
     sums = jnp.sum(total, axis=1, keepdims=True)
-    along, left = coefficients(
-        [jnp.broadcast_to(sums[i : i + 1, :], (ROWS, LANES)) for i in range(2 * ITERS)]
-    )
+    moments = [jnp.broadcast_to(sums[i : i + 1, :], (ROWS, LANES)) for i in range(2 * ITERS - 1)]
+    step, residual, direction, image, norm_now = coefficients(moments)
+    rest = energy_rest(direction, image, moments)
+    before, ahead, left, drop = [], [], [], []
     for c in range(chunks):
-        value = add_up([along[j] * basis_v[j, c] for j in range(ITERS)])
-        step_ref[pl.ds(c, FIELDS, stride=chunks), :] = value[0:FIELDS]
-        value = add_up([left[j] * basis_q[j, c] for j in range(ITERS + 1)])
-        residual_ref[pl.ds(c, FIELDS, stride=chunks), :] = value[0:FIELDS]
+        before.append(add_up([step[j] * basis_v[j, c] for j in range(ITERS - 1)]))
+        ahead.append(add_up([direction[j] * basis_v[j, c] for j in range(ITERS)]))
+        left.append(add_up([residual[j] * basis_q[j, c] for j in range(ITERS)]))
+        drop.append(add_up([image[j] * basis_q[j, c] for j in range(ITERS + 1)]))
+    sent(whole)
+    arrived(whole)
+    total = whole_send[...] + add_up([whole_recv[n] for n in range(len(whole_near))])
+    energy = jnp.broadcast_to(jnp.sum(total, axis=1, keepdims=True), (ROWS, LANES))
+    length = norm_now / (rest + direction[-1] * image[-1] * energy)
+    for c in range(chunks):
+        rows = pl.ds(c, FIELDS, stride=chunks)
+        step_ref[0, rows, :] = before[c][0:FIELDS]
+        step_ref[1, rows, :] = (length * ahead[c])[0:FIELDS]
+        residual_ref[0, rows, :] = left[c][0:FIELDS]
+        residual_ref[1, rows, :] = (-length * drop[c])[0:FIELDS]
 
 
 def local(mesh_shape, body_load, proximal, contact_blocks, slacks, dual_rows, first_body, second_body, border_bodies):
@@ -529,7 +553,7 @@
     f32, bf16, i32 = jnp.float32, jnp.bfloat16, jnp.int32
     vmem = pltpu.VMEM
     dma = pltpu.SemaphoreType.DMA
-    parts, wholes = ny * ys - 1, 2 * zs - 1
+    parts, wholes = ny * ys, 2 * zs - 1
     pair_rows = PAIR_ROWS * SPLITS
     operands = (
         body_load.reshape(FIELDS * chunks, LANES),
@@ -578,6 +602,10 @@
         vmem((parts, 1, LANES), f32),
         vmem((1, LANES), f32),
         vmem((wholes, 1, LANES), f32),
+        vmem((1, LANES), f32),
+        vmem((parts, 1, LANES), f32),
+        vmem((1, LANES), f32),
+        vmem((wholes, 1, LANES), f32),
         dma((8,)),
         dma((8,)),
         dma((ITERS, 8)),
@@ -588,17 +616,22 @@
         dma((parts,)),
         dma((wholes,)),
         dma((wholes,)),
+        dma((parts,)),
+        dma((parts,)),
+        dma((wholes,)),
+        dma((wholes,)),
     ]
     step, residual = pl.pallas_call(
         functools.partial(kernel, (nx, ny, ys, zs)),
-        out_shape=[jax.ShapeDtypeStruct((FIELDS * chunks, LANES), f32)] * 2,
-        in_specs=[pl.BlockSpec(memory_space=pl.ANY)] * 8,
+        out_shape=[jax.ShapeDtypeStruct((2, FIELDS * chunks, LANES), f32)] * 2,
+        in_specs=[pl.BlockSpec(memory_space=pltpu.HBM)] * 8,
         out_specs=[pl.BlockSpec(memory_space=pltpu.VMEM)] * 2,
         scratch_shapes=scratch,
         compiler_params=pltpu.CompilerParams(
             collective_id=0, has_side_effects=True, vmem_limit_bytes=56 * 1024 * 1024
         ),
     )(*operands)
+    step, residual = step[0] + step[1], residual[0] + residual[1]
     return step.reshape(body_load.shape), residual.reshape(body_load.shape)
 
 

time: 51.9 us -> 50.9 us (0.981)
  local copies, waits for them, and re-layouts: 1.92 us -> 0 us
  other arithmetic: 0 us -> 1.37 us
    unnamed x4 -> x0, local copies, waits for them, and re-layouts: 1.92 us -> none
    add x0 -> x1, other arithmetic: none -> 1.37 us  [local(): step, residual = (step[0] + step[1], residual[0] + residual[1])]
    pallas_call x1, Pallas kernels: 49.2 us -> 48.7 us  [local(): pl.pallas_call(functools.partial(kernel, (nx, ny, ys, zs)), out_shape=[ja...]
where the time goes in v3:
time: 50.9 us; the launch traced here: 50.7 us
  Pallas kernels  48.7 us (96%)
  other arithmetic  1.37 us (3%)
  between operations  0.64 us (1%)
    pallas_call x1, Pallas kernels, local(): pl.pallas_call(functools.partial(kernel, (nx, ny, ys, zs)), out_shape=[ja...  48.7 us
    add x1, other arithmetic, local(): step, residual = (step[0] + step[1], residual[0] + residual[1])  1.37 us

profile of v3, /device:TPU:1, one launch (start us, length us, event | category | flops | bytes accessed | tf_op | source)
XLA Modules:
  0.0 50.7 jit_solution(2730825236778588025)
XLA Ops:
  0.6 48.7 %shard_map.95 = (f32[2,24,128]{2,1,0:T(8,128)}, f32[2,24,128]{2,1,0:T(8,128)}) custom-call(f32[24,128]{1,0:T(8,128)} %bitcast.15, f32[24,128]{1,0:T(8,128)} %bitcast.16, f32[72,16,128]{2,1,0:T(8,128)} %bitcast.10, f32[6,16,128]{2,1,0:T(8,128)} %bitcast.11, f32[6,16,128]{2,1,0:T(8,128)} %bitcast.12, s32[16,128]{1,0:T(8,128)} %bitcast.17, s32[16,128]{1,0:T(8,128)} %bitcast.18, ...), custom_call_target="tpu_custom_call" | custom-call | tf_op jit(solution)/shard_map/pallas_call | solution.py:624
  49.3 1.4 %slice_add_fusion = (f32[1,24,128]{2,1,0:T(8,128)}, f32[1,24,128]{2,1,0:T(8,128)}) fusion(f32[2,24,128]{2,1,0:T(8,128)} %get-tuple-element.5, f32[2,24,128]{2,1,0:T(8,128)} %get-tuple-element.4), kind=kLoop, calls=%fused_computation | loop fusion | flops 6144 | bytes 73728 | tf_op jit(solution)/shard_map/add | solution.py:634

commit v4 on v3

--- a/solution.py
+++ b/solution.py
@@ -11,7 +11,9 @@
 LANES = 128
 ROWS = 8
 SPAN = 256
+HALO_SPANS = 2 * LANES // SPAN
 SPLITS = 3
+LOOP_SPLITS = 3
 FIELDS = 6
 PAIRS = [(a, b) for a in range(FIELDS) for b in range(a, FIELDS)]
 PAIR_ROWS = 24
@@ -26,18 +28,18 @@
 
 
 def add_up(values):
-    total = values[0]
-    for value in values[1:]:
-        total = total + value
-    return total
-
-
-def split_terms(values):
+    while len(values) > 1:
+        pairs = [a + b for a, b in zip(values[::2], values[1::2])]
+        values = pairs + values[len(pairs) * 2 :]
+    return values[0]
+
+
+def split_terms(values, splits):
     terms = []
-    for number in range(SPLITS):
+    for number in range(splits):
         term = values.astype(jnp.bfloat16).astype(jnp.float32)
         terms.append(term)
-        if number + 1 < SPLITS:
+        if number + 1 < splits:
             values = values - term
     return terms
 
@@ -130,7 +132,7 @@
     load_hbm, prox_hbm, block_hbm, slack_hbm, dual_hbm, first_hbm, second_hbm, border_hbm,
     step_ref, residual_ref,
     load_in, prox_in, block_in, slack_in, dual_in, first_in, second_in, border_in, in_sem,
-    g, hot1, hot2, hotb, span1, span2, spanb, laneb, chunkb, border_pad,
+    g, cross, hot1, hot2, hotb, span1, span2, spanb, laneb, chunkb, border_pad,
     left1, left2, left_halo, leftb, spread, spread_first, spread_pairs, spread_pairs_first,
     basis_v, basis_q, prox, inverse, diag, returned, columns,
     diag_send, diag_recv, fore_send, fore_recv, back_send, back_recv,
@@ -144,6 +146,7 @@
     chunks = load_in.shape[0] // FIELDS
     spans = chunks * LANES // SPAN
     tiles = first_in.shape[0]
+    HALO = range(spans, spans + HALO_SPANS)
     f32, bf16 = jnp.float32, jnp.bfloat16
     gx, gy = lax.axis_index("gx"), lax.axis_index("gy")
     z_at, y_at, core = gx // (2 * ys), (gx // 2) % ys, gx % 2
@@ -193,8 +196,8 @@
                 same, 1.0, 0.0
             ).astype(bf16)
 
-    def write_terms(target, values, masks):
-        pieces = [jnp.where(mask, t, 0.0) for t in split_terms(values) for mask in masks]
+    def write_terms(target, values, masks, splits):
+        pieces = [jnp.where(mask, t, 0.0) for t in split_terms(values, splits) for mask in masks]
         if (len(pieces) * values.shape[1]) % 16:
             pieces.append(jnp.zeros((values.shape[0], ROWS, LANES), f32))
         packed = jnp.concatenate(pieces, axis=1).astype(bf16)
@@ -202,16 +205,16 @@
             target[0 : packed.shape[1], s * LANES : (s + 1) * LANES] = packed[s]
         return packed.shape[1]
 
-    def read_terms(product, rows, masks):
+    def read_terms(product, rows, masks, splits):
         result = []
         for mask in range(masks):
             total = add_up(
                 [
                     product[(n * masks + mask) * rows : (n * masks + mask + 1) * rows]
-                    for n in range(SPLITS)
+                    for n in range(splits)
                 ]
             )
-            result.extend([total[:, :LANES], total[:, LANES:]])
+            result.extend([total[:, at : at + LANES] for at in range(0, SPAN, LANES)])
         return result
 
     def arrange(slots, place_of):
@@ -297,15 +300,15 @@
             g[r * 12 + j] = block_in[r * 12 + j] * root[r]
     pair_products(6, spread_pairs)
     pair_values = spread_pairs[...].reshape(tiles, PAIR_ROWS, LANES)
-    rows = write_terms(left_halo, pair_values, masks_of(span2, PAIR_ROWS, [spans]))
-    halves = read_terms(dot(left_halo[0:rows, :], hot2[...]), PAIR_ROWS, 1)
+    rows = write_terms(left_halo, pair_values, masks_of(span2, PAIR_ROWS, HALO), SPLITS)
+    halves = read_terms(dot(left_halo[0:rows, :], hot2[...]), PAIR_ROWS, HALO_SPANS, SPLITS)
     for half in range(2):
         diag_send[half] = halves[half]
     pl.semaphore_wait(barrier, len(everyone))
     copies = exchange(diag_send, diag_recv, diag_ssem, diag_rsem, forward)
 
-    rows = write_terms(left2, pair_values, masks_of(span2, PAIR_ROWS, range(spans)))
-    local2 = read_terms(dot(left2[0:rows, :], hot2[...]), PAIR_ROWS, spans)
+    rows = write_terms(left2, pair_values, masks_of(span2, PAIR_ROWS, range(spans)), SPLITS)
+    local2 = read_terms(dot(left2[0:rows, :], hot2[...]), PAIR_ROWS, spans, SPLITS)
     for r in range(6):
         for j in range(6):
             g[r * 12 + j] = block_in[r * 12 + j] * root[r]
@@ -315,9 +318,12 @@
         row = first_in[s : s + 1, :]
         span1[s] = jnp.broadcast_to(row // SPAN, (ROWS, LANES))
         build_hot(hot1, row, s * LANES)
+    for j in range(6):
+        for a in range(6):
+            cross[j * 6 + a] = add_up([g[r * 12 + 6 + j] * g[r * 12 + a] for r in range(6)])
     pair_values = spread_pairs_first[...].reshape(tiles, PAIR_ROWS, LANES)
-    rows = write_terms(left1, pair_values, masks_of(span1, PAIR_ROWS, range(spans)))
-    local1 = read_terms(dot(left1[0:rows, :], hot1[...]), PAIR_ROWS, spans)
+    rows = write_terms(left1, pair_values, masks_of(span1, PAIR_ROWS, range(spans)), SPLITS)
+    local1 = read_terms(dot(left1[0:rows, :], hot1[...]), PAIR_ROWS, spans, SPLITS)
     for c in range(chunks):
         diag[c] = local1[c] + local2[c]
     loads[5].wait()
@@ -354,8 +360,8 @@
     halves = arrange(lambda k: diag_recv[k], reverse)
     for half in range(2):
         returned[half] = halves[half]
-    rows = write_terms(leftb, returned[...], masks_of(spanb, PAIR_ROWS, range(spans)))
-    localb = read_terms(dot(leftb[0:rows, :], hotb[...]), PAIR_ROWS, spans)
+    rows = write_terms(leftb, returned[...], masks_of(spanb, PAIR_ROWS, range(spans)), SPLITS)
+    localb = read_terms(dot(leftb[0:rows, :], hotb[...]), PAIR_ROWS, spans, SPLITS)
     entries = {}
     for c in range(chunks):
         spread_pairs[pl.ds(c, PAIR_ROWS, stride=ROWS), :] = diag[c] + localb[c]
@@ -420,13 +426,12 @@
         back_refs = (back_send.at[k], back_recv.at[k], back_ssem.at[k], back_rsem.at[k], forward)
         fore = exchange(*fore_refs, FAR)
         u1 = gather_fields(lambda f, n: basis_v[k, n, f : f + 1, :], lane1, chunk1, 0, chunks)
-        strain = [add_up([g[r * 12 + j] * u1[j] for j in range(6)]) for r in range(6)]
         for j in range(6):
-            value = add_up([g[r * 12 + 6 + j] * strain[r] for r in range(6)])
+            value = add_up([cross[j * 6 + a] * u1[a] for a in range(6)])
             spread[pl.ds(j, tiles, stride=ROWS), :] = value
         pulls = spread[...].reshape(tiles, ROWS, LANES)
-        rows = write_terms(left_halo, pulls, masks_of(span2, ROWS, [spans]))
-        halves = read_terms(dot(left_halo[0:rows, :], hot2[...]), ROWS, 1)
+        rows = write_terms(left_halo, pulls, masks_of(span2, ROWS, HALO), LOOP_SPLITS)
+        halves = read_terms(dot(left_halo[0:rows, :], hot2[...]), ROWS, HALO_SPANS, LOOP_SPLITS)
         for half in range(2):
             back_send[k, half] = halves[half]
         back = exchange(*back_refs, FAR)
@@ -441,14 +446,18 @@
         here = chunk2 < chunks
         u2 = [jnp.where(here, value, 0.0) for value in u2]
         strain = [
-            strain[r] + add_up([g[r * 12 + 6 + j] * u2[j] for j in range(6)]) for r in range(6)
+            add_up(
+                [g[r * 12 + j] * u1[j] for j in range(6)]
+                + [g[r * 12 + 6 + j] * u2[j] for j in range(6)]
+            )
+            for r in range(6)
         ]
         for j in range(6):
             value = add_up([g[r * 12 + 6 + j] * strain[r] for r in range(6)])
             spread[pl.ds(j, tiles, stride=ROWS), :] = value
         pulls = spread[...].reshape(tiles, ROWS, LANES)
-        rows = write_terms(left2, pulls, masks_of(span2, ROWS, range(spans)))
-        image = read_terms(dot(left2[0:rows, :], hot2[...]), ROWS, spans)
+        rows = write_terms(left2, pulls, masks_of(span2, ROWS, range(spans)), LOOP_SPLITS)
+        image = read_terms(dot(left2[0:rows, :], hot2[...]), ROWS, spans, LOOP_SPLITS)
         image = [image[c] + prox[c] * v_now[c] - q_now[c] for c in range(chunks)]
         pushes = [add_up([g[r * 12 + j] * strain[r] for r in range(6)]) for j in range(6)]
         if k == 0:
@@ -474,28 +483,26 @@
         arrived(fore)
         beyond = arrange(lambda s: fore_recv[k, s], forward)
         u2 = gather_fields(lambda f, n: beyond[n][f : f + 1, :], lane2, chunk2, chunks, 2)
-        more = [
-            add_up([g[r * 12 + 6 + j] * u2[j] for j in range(6)]) for r in range(6)
-        ]
-        for j in range(6):
-            value = pushes[j] + add_up([g[r * 12 + j] * more[r] for r in range(6)])
-            spread_first[pl.ds(j, tiles, stride=ROWS), :] = value
+        for a in range(6):
+            value = pushes[a] + add_up([cross[j * 6 + a] * u2[j] for j in range(6)])
+            spread_first[pl.ds(a, tiles, stride=ROWS), :] = value
         if k == ITERS - 1:
+            more = [add_up([g[r * 12 + 6 + j] * u2[j] for j in range(6)]) for r in range(6)]
             energy = add_up([(strain[r] + more[r]) * (strain[r] + more[r]) for r in range(6)])
             energy = add_up([energy[t : t + ROWS] for t in range(0, tiles, ROWS)])
             energy = energy + add_up([prox[c] * v_now[c] * v_now[c] for c in range(chunks)])
             part_send[...] = sum_rows(energy)[0:1]
             part = broadcast_all(part_send, part_recv, part_ssem, part_rsem, part_near)
         values = spread_first[...].reshape(tiles, ROWS, LANES)
-        rows = write_terms(left1, values, masks_of(span1, ROWS, range(spans)))
-        pushed = read_terms(dot(left1[0:rows, :], hot1[...]), ROWS, spans)
+        rows = write_terms(left1, values, masks_of(span1, ROWS, range(spans)), LOOP_SPLITS)
+        pushed = read_terms(dot(left1[0:rows, :], hot1[...]), ROWS, spans, LOOP_SPLITS)
         image = [image[c] + pushed[c] for c in range(chunks)]
         arrived(back)
         late = back
         halves = arrange(lambda s: back_recv[k, s], reverse)
         values = jnp.concatenate([(halves[h] + pulled[h])[None] for h in range(2)], axis=0)
-        rows = write_terms(leftb, values, masks_of(spanb, ROWS, range(spans)))
-        added = read_terms(dot(leftb[0:rows, :], hotb[...]), ROWS, spans)
+        rows = write_terms(leftb, values, masks_of(spanb, ROWS, range(spans)), LOOP_SPLITS)
+        added = read_terms(dot(leftb[0:rows, :], hotb[...]), ROWS, spans, LOOP_SPLITS)
         q_next = [image[c] + added[c] for c in range(chunks)]
         for c in range(chunks):
             basis_q[k + 1, c] = q_next[c]
@@ -568,6 +575,7 @@
     scratch = [vmem(a.shape, a.dtype) for a in operands] + [
         dma((8,)),
         vmem((12 * FIELDS, tiles, LANES), f32),
+        vmem((FIELDS * FIELDS, tiles, LANES), f32),
         vmem((contacts, SPAN), bf16),
         vmem((contacts, SPAN), bf16),
         vmem((2 * LANES, SPAN), bf16),
@@ -579,7 +587,7 @@
         vmem((ROWS, LANES), i32),
         vmem((pair_rows * spans, contacts), bf16),
         vmem((pair_rows * spans, contacts), bf16),
-        vmem((pair_rows + ROWS, contacts), bf16),
+        vmem((pair_rows * HALO_SPANS + ROWS, contacts), bf16),
         vmem((pair_rows * spans, 2 * LANES), bf16),
         vmem((tiles * ROWS, LANES), f32),
         vmem((tiles * ROWS, LANES), f32),
@@ -628,9 +636,9 @@
         out_specs=[pl.BlockSpec(memory_space=pltpu.VMEM)] * 2,
         scratch_shapes=scratch,
         compiler_params=pltpu.CompilerParams(
-            collective_id=0, has_side_effects=True, vmem_limit_bytes=56 * 1024 * 1024
+            collective_id=0, has_side_effects=True, vmem_limit_bytes=32 * 1024 * 1024
         ),
-    )(*operands)
+    )(*[pltpu.with_memory_space_constraint(a, pltpu.HBM) for a in operands])
     step, residual = step[0] + step[1], residual[0] + residual[1]
     return step.reshape(body_load.shape), residual.reshape(body_load.shape)
 

time: 50.9 us -> 49.4 us (0.971)
  other arithmetic: 1.37 us -> 0.61 us
  Pallas kernels: 48.7 us -> 48 us
    add x1, other arithmetic: 1.37 us -> 0.61 us  [local(): step, residual = (step[0] + step[1], residual[0] + residual[1])]
    pallas_call x1, Pallas kernels: 48.7 us -> 48 us  [local(): pl.pallas_call(functools.partial(kernel, (nx, ny, ys, zs)), out_shape=[ja...]
where the time goes in v4:
time: 49.4 us; the launch traced here: 49.2 us
  Pallas kernels  48 us (97%)
  between operations  0.64 us (1%)
  other arithmetic  0.61 us (1%)
    pallas_call x1, Pallas kernels, local(): pl.pallas_call(functools.partial(kernel, (nx, ny, ys, zs)), out_shape=[ja...  48 us

profile of v4, /device:TPU:1, one launch (start us, length us, event | category | flops | bytes accessed | tf_op | source)
XLA Modules:
  0.0 49.2 jit_solution(4826429920403452856)
XLA Ops:
  0.6 48.0 %shard_map.95 = (f32[2,24,128]{2,1,0:T(8,128)S(1)}, f32[2,24,128]{2,1,0:T(8,128)S(1)}) custom-call(f32[24,128]{1,0:T(8,128)} %bitcast.15, f32[24,128]{1,0:T(8,128)} %bitcast.16, f32[72,16,128]{2,1,0:T(8,128)} %bitcast.10, f32[6,16,128]{2,1,0:T(8,128)} %bitcast.11, f32[6,16,128]{2,1,0:T(8,128)} %bitcast.12, s32[16,128]{1,0:T(8,128)} %bitcast.17, ...), custom_call_target="tpu_custom_call" | custom-call | tf_op jit(solution)/shard_map/pallas_call | solution.py:632
  48.6 0.6 %slice_add_fusion = (f32[1,24,128]{2,1,0:T(8,128)}, f32[1,24,128]{2,1,0:T(8,128)}) fusion(f32[2,24,128]{2,1,0:T(8,128)S(1)} %get-tuple-element.5, f32[2,24,128]{2,1,0:T(8,128)S(1)} %get-tuple-element.4), kind=kLoop, calls=%fused_computation | loop fusion | flops 6144 | bytes 73728 | tf_op jit(solution)/shard_map/add | solution.py:642

commit v5 on v4

--- a/solution.py
+++ b/solution.py
@@ -143,7 +143,7 @@
     part_ssem, part_rsem, whole_ssem, whole_rsem,
 ):
     nx, ny, ys, zs = sizes
-    chunks = load_in.shape[0] // FIELDS
+    chunks = load_hbm.shape[0] // FIELDS
     spans = chunks * LANES // SPAN
     tiles = first_in.shape[0]
     HALO = range(spans, spans + HALO_SPANS)
@@ -178,8 +178,8 @@
             (dual_hbm, dual_in),
             (first_hbm, first_in),
             (border_hbm, border_in),
-            (load_hbm, load_in),
-            (prox_hbm, prox_in),
+            (load_hbm, load_in.at[0 : load_hbm.shape[0]]),
+            (prox_hbm, prox_in.at[0 : prox_hbm.shape[0]]),
         )
     ):
         loads.append(pltpu.make_async_copy(source, target, in_sem.at[number]))
@@ -572,7 +572,9 @@
         second_body.reshape(tiles, LANES),
         border_bodies.reshape(border_bodies.shape[2:]),
     )
-    scratch = [vmem(a.shape, a.dtype) for a in operands] + [
+    field_rows = ROWS * chunks
+    scratch = [vmem((field_rows, LANES), f32)] * 2
+    scratch += [vmem(a.shape, a.dtype) for a in operands[2:]] + [
         dma((8,)),
         vmem((12 * FIELDS, tiles, LANES), f32),
         vmem((FIELDS * FIELDS, tiles, LANES), f32),
@@ -596,7 +598,7 @@
         vmem((ITERS, chunks, ROWS, LANES), f32),
         vmem((ITERS + 1, chunks, ROWS, LANES), f32),
         vmem((chunks, ROWS, LANES), f32),
-        vmem((FIELDS * chunks * ROWS, LANES), f32),
+        vmem((FIELDS * chunks * ROWS + 8 * ROWS, LANES), f32),
         vmem((chunks, PAIR_ROWS, LANES), f32),
         vmem((2, PAIR_ROWS, LANES), f32),
         vmem((FIELDS, 2, ROWS, LANES), f32),
@@ -631,7 +633,7 @@
     ]
     step, residual = pl.pallas_call(
         functools.partial(kernel, (nx, ny, ys, zs)),
-        out_shape=[jax.ShapeDtypeStruct((2, FIELDS * chunks, LANES), f32)] * 2,
+        out_shape=[jax.ShapeDtypeStruct((2, field_rows, LANES), f32)] * 2,
         in_specs=[pl.BlockSpec(memory_space=pltpu.HBM)] * 8,
         out_specs=[pl.BlockSpec(memory_space=pltpu.VMEM)] * 2,
         scratch_shapes=scratch,
@@ -639,6 +641,7 @@
             collective_id=0, has_side_effects=True, vmem_limit_bytes=32 * 1024 * 1024
         ),
     )(*[pltpu.with_memory_space_constraint(a, pltpu.HBM) for a in operands])
+    step, residual = step[:, : FIELDS * chunks], residual[:, : FIELDS * chunks]
     step, residual = step[0] + step[1], residual[0] + residual[1]
     return step.reshape(body_load.shape), residual.reshape(body_load.shape)
 

time: 49.4 us -> 49.4 us (level)
  no operation moved by 1% of the time
where the time goes in v5:
time: 49.4 us; the launch traced here: 49.2 us
  Pallas kernels  48 us (97%)
  between operations  0.64 us (1%)
  other arithmetic  0.61 us (1%)
    pallas_call x1, Pallas kernels, local(): pl.pallas_call(functools.partial(kernel, (nx, ny, ys, zs)), out_shape=[ja...  48 us

profile of v5, /device:TPU:1, one launch (start us, length us, event | category | flops | bytes accessed | tf_op | source)
XLA Modules:
  0.0 49.2 jit_solution(14487250449179573795)
XLA Ops:
  0.6 48.0 %shard_map.95 = (f32[2,32,128]{2,1,0:T(8,128)S(1)}, f32[2,32,128]{2,1,0:T(8,128)S(1)}) custom-call(f32[24,128]{1,0:T(8,128)} %bitcast.15, f32[24,128]{1,0:T(8,128)} %bitcast.16, f32[72,16,128]{2,1,0:T(8,128)} %bitcast.10, f32[6,16,128]{2,1,0:T(8,128)} %bitcast.11, f32[6,16,128]{2,1,0:T(8,128)} %bitcast.12, s32[16,128]{1,0:T(8,128)} %bitcast.17, ...), custom_call_target="tpu_custom_call" | custom-call | tf_op jit(solution)/shard_map/pallas_call | solution.py:634
  48.6 0.6 %slice_add_fusion = (f32[1,24,128]{2,1,0:T(8,128)}, f32[1,24,128]{2,1,0:T(8,128)}) fusion(f32[2,32,128]{2,1,0:T(8,128)S(1)} %get-tuple-element.5, f32[2,32,128]{2,1,0:T(8,128)S(1)} %get-tuple-element.4), kind=kLoop, calls=%fused_computation | loop fusion | flops 6144 | bytes 73728 | tf_op jit(solution)/shard_map/add | solution.py:645
